TPU v7x, 128 devices: a whole 4x4x4 slice. The times are simulated.
128 devices in a mesh: seq: 32 (over y, z, core), head: 4 (over x).
Axes of the slice: x: 4, y: 4, z: 4, core: 2. Of those that a mesh axis runs over, the one named last changes fastest.
Arguments:
- queries: bfloat16 [32768, 2048], P('seq', 'head'), may hold values from -8 to 8
- key_rows: bfloat16 [32768, 2048], P('seq', 'head'), may hold values from -8 to 8
- value_rows: bfloat16 [32768, 2048], P('seq', 'head'), may hold values from -6 to 6
- grad_out: bfloat16 [32768, 2048], P('seq', 'head'), may hold values from -6 to 6
- cluster_ids: int32 [32768, 16], P('seq', 'head'), may hold values from 0 to 63, as said below
Outputs:
- attended: bfloat16 [32768, 2048], P('seq', 'head')
- grad_query: bfloat16 [32768, 2048], P('seq', 'head')
- grad_key: bfloat16 [32768, 2048], P('seq', 'head')
- grad_value: bfloat16 [32768, 2048], P('seq', 'head')
Inputs may be any that keep to these rules, and one draw needn't show every extreme that they name: `cluster_ids`: among the 1024 tokens of one index of seq, at most 24 carry one cluster number in one head's column; in every head some cluster number is carried by exactly 24 tokens of every index of seq.
All inputs are finite; a program needn't handle non-finite values.
Results may differ from a plain program's by a relative error of at most 0.012.
The roundings to bfloat16 on the way count: a program that leaves them out, or rounds other values in their place, can miss the bound.
Values may be sent and summed in bfloat16 or wider, within the bound.
No kernel may reach another device: no remote copies, remote signals or barrier semaphores. Data moves between devices by JAX's collectives and lax.ppermute only.
A program may use at most 64 MiB of HBM per device.

v0:
```python
import jax
import jax.numpy as jnp
from jax import lax
from jax.sharding import PartitionSpec as P

WINDOW = 512


def probabilities(query_part, key_part, places, factor):
    scores = (
        lax.dot_general(
            query_part, key_part, (((1,), (1,)), ((), ())), preferred_element_type=jnp.float32
        )
        * factor
    )
    allowed = (places[None, :] <= places[:, None]) & (places[None, :] >= 0)
    allowed = allowed | jnp.eye(places.shape[0], dtype=bool)
    scores = jnp.where(allowed, scores, -jnp.inf)
    row_max = jnp.max(scores, axis=1, keepdims=True)
    weights = jnp.exp(scores - row_max)
    return weights / jnp.sum(weights, axis=1, keepdims=True)


def gradients(shares, query_part, key_part, value_part, attended_part, upstream, factor):
    coarse = shares.astype(jnp.bfloat16)
    through = lax.dot_general(
        upstream, value_part, (((1,), (1,)), ((), ())), preferred_element_type=jnp.float32
    )
    row_dot = jnp.sum(
        upstream.astype(jnp.float32) * attended_part.astype(jnp.float32), axis=1, keepdims=True
    )
    slope = (shares * (through - row_dot)).astype(jnp.bfloat16)
    value_grad = lax.dot_general(
        coarse, upstream, (((0,), (0,)), ((), ())), preferred_element_type=jnp.float32
    ).astype(jnp.bfloat16)
    query_grad = (factor * jnp.dot(slope, key_part, preferred_element_type=jnp.float32)).astype(
        jnp.bfloat16
    )
    key_grad = (
        factor
        * lax.dot_general(
            slope, query_part, (((0,), (0,)), ((), ())), preferred_element_type=jnp.float32
        )
    ).astype(jnp.bfloat16)
    return (query_grad, key_grad, value_grad)


def on_device(queries, key_rows, value_rows, grad_out, cluster_ids):
    tokens_here, heads_here = cluster_ids.shape
    head_size = queries.shape[1] // heads_here
    factor = float(head_size) ** (-0.5)
    seq_count = lax.axis_size("seq")
    slot_count = 3 * WINDOW // (2 * seq_count)
    clusters_here = tokens_here // WINDOW
    clusters = clusters_here * seq_count
    groups = heads_here * clusters_here
    capacity = seq_count * slot_count
    head_rows = clusters_here * capacity
    token_line = jnp.arange(tokens_here, dtype=jnp.int32)
    member_marks = (
        cluster_ids[:, :, None] == jnp.arange(clusters, dtype=jnp.int32)[None, None, :]
    ).astype(jnp.bfloat16)
    lower_table = (token_line[None, :] < token_line[:, None]).astype(jnp.bfloat16)
    before = jnp.dot(
        lower_table,
        member_marks.reshape(tokens_here, heads_here * clusters),
        preferred_element_type=jnp.float32,
    )
    ranking = jnp.sum(
        before.reshape(tokens_here, heads_here, clusters) * member_marks.astype(jnp.float32), axis=2
    ).astype(jnp.int32)
    owners = cluster_ids // clusters_here
    within = cluster_ids % clusters_here
    local_slot = (within * seq_count + owners) * slot_count + ranking
    slot_line = jnp.arange(head_rows, dtype=jnp.int32)
    hits = local_slot.T[:, None, :] == slot_line[None, :, None]
    selector = hits.astype(jnp.bfloat16)
    source_token = jnp.max(jnp.where(hits, token_line[None, None, :], -1), axis=2)
    anchor = lax.axis_index("seq") * tokens_here
    placed = jnp.where(source_token >= 0, source_token + anchor, -1).reshape(
        groups, seq_count, slot_count
    )
    stacked = jnp.concatenate(
        [
            field.reshape(tokens_here, heads_here, head_size)
            for field in (queries, key_rows, value_rows, grad_out)
        ],
        axis=2,
    )
    arranged = jnp.einsum(
        "hbt,thf->hbf", selector, stacked, preferred_element_type=jnp.float32
    ).astype(jnp.bfloat16)

    def buffer_of(index):
        return arranged[:, :, index * head_size : (index + 1) * head_size].reshape(
            groups, seq_count, slot_count, head_size
        )

    query_buffer = buffer_of(0)
    key_buffer = buffer_of(1)
    value_buffer = buffer_of(2)
    upstream_buffer = buffer_of(3)

    def forward_one(bundle):
        query_part, key_part, value_part, places = bundle
        shares = probabilities(query_part, key_part, places, factor)
        return jnp.dot(
            shares.astype(jnp.bfloat16), value_part, preferred_element_type=jnp.float32
        ).astype(jnp.bfloat16)

    def backward_one(bundle):
        query_part, key_part, value_part, places, attended_part, upstream = bundle
        shares = probabilities(query_part, key_part, places, factor)
        return gradients(shares, query_part, key_part, value_part, attended_part, upstream, factor)

    arrived = (
        lax.all_to_all(query_buffer, "seq", split_axis=1, concat_axis=1, tiled=True),
        lax.all_to_all(key_buffer, "seq", split_axis=1, concat_axis=1, tiled=True),
        lax.all_to_all(value_buffer, "seq", split_axis=1, concat_axis=1, tiled=True),
        lax.all_to_all(placed, "seq", split_axis=1, concat_axis=1, tiled=True),
    )
    query_owned = arrived[0].reshape(groups, capacity, head_size)
    key_owned = arrived[1].reshape(groups, capacity, head_size)
    value_owned = arrived[2].reshape(groups, capacity, head_size)
    places_owned = arrived[3].reshape(groups, capacity)
    attended_owned = lax.map(forward_one, (query_owned, key_owned, value_owned, places_owned))
    attended_back = lax.all_to_all(
        attended_owned.reshape(groups, seq_count, slot_count, head_size),
        "seq",
        split_axis=1,
        concat_axis=1,
        tiled=True,
    )
    upstream_owned = lax.all_to_all(
        upstream_buffer, "seq", split_axis=1, concat_axis=1, tiled=True
    ).reshape(groups, capacity, head_size)
    owned_grads = lax.map(
        backward_one,
        (query_owned, key_owned, value_owned, places_owned, attended_owned, upstream_owned),
    )
    returned = (
        lax.all_to_all(
            owned_grads[0].reshape(groups, seq_count, slot_count, head_size),
            "seq",
            split_axis=1,
            concat_axis=1,
            tiled=True,
        ),
        lax.all_to_all(
            owned_grads[1].reshape(groups, seq_count, slot_count, head_size),
            "seq",
            split_axis=1,
            concat_axis=1,
            tiled=True,
        ),
        lax.all_to_all(
            owned_grads[2].reshape(groups, seq_count, slot_count, head_size),
            "seq",
            split_axis=1,
            concat_axis=1,
            tiled=True,
        ),
    )
    results = (attended_back, returned[0], returned[1], returned[2])
    gathered_back = jnp.concatenate(
        [field.reshape(heads_here, head_rows, head_size) for field in results], axis=2
    )
    unpacked = jnp.einsum(
        "hbt,hbf->thf", selector, gathered_back, preferred_element_type=jnp.float32
    ).astype(jnp.bfloat16)

    def output_of(index):
        return unpacked[:, :, index * head_size : (index + 1) * head_size].reshape(
            tokens_here, heads_here * head_size
        )

    return (output_of(0), output_of(1), output_of(2), output_of(3))


def solution(mesh):
    in_specs = (
        P("seq", "head"),
        P("seq", "head"),
        P("seq", "head"),
        P("seq", "head"),
        P("seq", "head"),
    )
    out_specs = (P("seq", "head"), P("seq", "head"), P("seq", "head"), P("seq", "head"))
    return jax.shard_map(
        on_device, mesh=mesh, in_specs=in_specs, out_specs=out_specs, check_vma=False
    )
```

profile of v0, /device:TPU:34, one launch (start us, length us, event | category | flops | bytes accessed | tf_op | source)
XLA Modules:
  0.0 381.7 jit_solution(8688926836411161201)
XLA Ops:
  3.3 3.9 %select_reduce_fusion = s32[4,1536]{1,0:T(4,128)S(1)} fusion(s32[4,1024]{1,0:T(4,128)S(1)} %fusion.91), kind=kLoop, calls=%fused_computation.64 | loop fusion | flops 18868224 | bytes 40960 | tf_op jit(solution)/shard_map/reduce_max | solution.py:78
  8.3 8.2 %all-to-all-start = ((s32[32,1,192]{2,1,0:T(1,128)}), s32[32,1,192]{2,1,0:T(1,128)S(1)}, u32[]{:S(2)}, u32[]{:S(2)}) async-start(s32[32,1,192]{2,1,0:T(1,128)} %reshape.140), calls=%async_computation | async-start | bytes 65536 | tf_op jit(solution)/shard_map/all_to_all | solution.py:120
  23.8 8.1 %fusion.67 = bf16[4,1536,512]{2,1,0:T(8,128)(2,1)S(1)} fusion(s32[4,1024]{1,0:T(4,128)S(1)} %fusion.91, bf16[1024,4,128]{2,0,1:T(8,128)(2,1)} %copy.68, bf16[1024,4,128]{2,0,1:T(8,128)(2,1)} %copy.67, bf16[1024,4,128]{2,0,1:T(8,128)(2,1)S(1)} %copy-done.5, bf16[1024,4,128]{2,0,1:T(8,128)(2,1)S(1)} %copy.65), kind=kOutput, calls=%fused_computation.77 | convolution fusion | flops 6468665344 | bytes 10502144 | tf_op jit(solution)/shard_map/hbt,thf->hbf/dot_general | solution.py:90
  31.9 3.0 fusion.98
  36.5 7.4 %all-to-all-start.1 = ((bf16[8,32,24,128]{3,2,0,1:T(8,128)(2,1)}), bf16[8,32,24,128]{3,2,0,1:T(8,128)(2,1)S(1)}, u32[]{:S(2)}, u32[]{:S(2)}) async-start(bf16[8,32,24,128]{3,2,0,1:T(8,128)(2,1)} %copy.69), calls=%async_computation.1 | async-start | bytes 3145728 | tf_op jit(solution)/shard_map/all_to_all | solution.py:117
  43.9 3.0 copy.71
  46.9 18.0 %all-to-all-done.1 = bf16[8,32,24,128]{3,2,0,1:T(8,128)(2,1)S(1)} async-done(((bf16[8,32,24,128]{3,2,0,1:T(8,128)(2,1)}), bf16[8,32,24,128]{3,2,0,1:T(8,128)(2,1)S(1)}, u32[]{:S(2)}, u32[]{:S(2)}) %all-to-all-start.1) | async-done | bytes 1572896 | tf_op jit(solution)/shard_map/all_to_all | solution.py:117
  64.9 6.6 %all-to-all-start.2 = ((bf16[8,32,24,128]{3,2,0,1:T(8,128)(2,1)}), bf16[8,32,24,128]{3,2,0,1:T(8,128)(2,1)}, u32[]{:S(2)}, u32[]{:S(2)}) async-start(bf16[8,32,24,128]{3,2,0,1:T(8,128)(2,1)} %copy.71), calls=%async_computation.2 | async-start | bytes 3145728 | tf_op jit(solution)/shard_map/all_to_all | solution.py:118
  71.6 3.0 copy.73
  74.6 18.2 %all-to-all-done.2 = bf16[8,32,24,128]{3,2,0,1:T(8,128)(2,1)} async-done(((bf16[8,32,24,128]{3,2,0,1:T(8,128)(2,1)}), bf16[8,32,24,128]{3,2,0,1:T(8,128)(2,1)}, u32[]{:S(2)}, u32[]{:S(2)}) %all-to-all-start.2) | async-done | bytes 1572896 | tf_op jit(solution)/shard_map/all_to_all | solution.py:118
  92.7 6.6 %all-to-all-start.3 = ((bf16[8,32,24,128]{3,2,0,1:T(8,128)(2,1)}), bf16[8,32,24,128]{3,2,0,1:T(8,128)(2,1)}, u32[]{:S(2)}, u32[]{:S(2)}) async-start(bf16[8,32,24,128]{3,2,0,1:T(8,128)(2,1)} %copy.73), calls=%async_computation.3 | async-start | bytes 3145728 | tf_op jit(solution)/shard_map/all_to_all | solution.py:119
  104.0 2.8 copy.72
  106.8 13.8 %all-to-all-done.3 = bf16[8,32,24,128]{3,2,0,1:T(8,128)(2,1)} async-done(((bf16[8,32,24,128]{3,2,0,1:T(8,128)(2,1)}), bf16[8,32,24,128]{3,2,0,1:T(8,128)(2,1)}, u32[]{:S(2)}, u32[]{:S(2)}) %all-to-all-start.3) | async-done | bytes 1572896 | tf_op jit(solution)/shard_map/all_to_all | solution.py:119
  120.6 5.9 %all-to-all-start.5 = ((bf16[8,32,24,128]{3,2,0,1:T(8,128)(2,1)}), bf16[8,32,24,128]{3,2,0,1:T(8,128)(2,1)S(1)}, u32[]{:S(2)}, u32[]{:S(2)}) async-start(bf16[8,32,24,128]{3,2,0,1:T(8,128)(2,1)} %copy.77), calls=%async_computation.5 | async-start | bytes 3145728 | tf_op jit(solution)/shard_map/all_to_all | solution.py:134
  126.5 2.8 copy.74
  129.6 30.5 %while.24 = (s32[]{:T(128)}, bf16[8,768,128]{2,1,0:T(8,128)(2,1)S(1)}, s32[8,768]{1,0:T(8,128)S(1)}, bf16[8,768,128]{2,1,0:T(8,128)(2,1)}, bf16[8,768,128]{2,1,0...) while((s32[]{:T(128)}, bf16[8,768,128]{2,1,0:T(8,128)(2,1)S(1)}, s32[8,768]{1,0:T(8,128)S(1)}, ...), condition=%wide.region_5.6_spmd, body=%wide.region_2.5_spmd.sunk | while | flops 309165312 | bytes 7903061 | solution.py:126
  129.6 1.8 fusion.123
  133.4 1.8 fusion.123
  137.2 1.8 fusion.123
  141.0 1.8 fusion.123
  144.8 1.8 fusion.123
  148.7 1.8 fusion.123
  152.5 1.8 fusion.123
  156.3 1.8 fusion.123
  164.5 86.1 %while.25 = (s32[]{:T(128)}, bf16[8,768,128]{2,1,0:T(8,128)(2,1)S(1)}, bf16[8,768,128]{2,1,0:T(8,128)(2,1)}, bf16[8,768,128]{2,1,0:T(8,128)(2,1)}, s32[8,768]{1,...) while((s32[]{:T(128)}, ...), condition=%wide.region_10.11_spmd, body=%wide.region_6.10_spmd.sunk | while | flops 765884928 | bytes 15387513 | solution.py:137
  164.5 1.8 fusion.136
  166.7 2.1 fusion.140
  171.6 2.1 fusion.139
  175.3 1.8 fusion.136
  177.4 2.1 fusion.140
  182.4 2.1 fusion.139
  186.0 1.8 fusion.136
  188.2 2.2 fusion.140
  193.1 2.1 fusion.139
  196.8 1.8 fusion.136
  199.0 2.1 fusion.140
  203.9 2.1 fusion.139
  207.6 1.8 fusion.136
  209.8 2.1 fusion.140
  214.7 2.1 fusion.139
  218.4 1.8 fusion.136
  220.5 2.1 fusion.140
  225.5 2.1 fusion.139
  229.1 1.8 fusion.136
  231.3 2.1 fusion.140
  236.2 2.1 fusion.139
  239.9 1.8 fusion.136
  242.1 2.1 fusion.140
  247.0 2.1 fusion.139
  252.2 7.5 %all-to-all-start.6 = ((bf16[8,32,24,128]{3,2,0,1:T(8,128)(2,1)}), bf16[8,32,24,128]{3,2,0,1:T(8,128)(2,1)S(1)}, u32[]{:S(2)}, u32[]{:S(2)}) async-start(bf16[8,32,24,128]{3,2,0,1:T(8,128)(2,1)} %copy.79), calls=%async_computation.6 | async-start | bytes 3145728 | tf_op jit(solution)/shard_map/all_to_all | solution.py:142
  259.7 3.0 copy.81
  262.7 18.0 %all-to-all-done.6 = bf16[8,32,24,128]{3,2,0,1:T(8,128)(2,1)S(1)} async-done(((bf16[8,32,24,128]{3,2,0,1:T(8,128)(2,1)}), bf16[8,32,24,128]{3,2,0,1:T(8,128)(2,1)S(1)}, u32[]{:S(2)}, u32[]{:S(2)}) %all-to-all-start.6) | async-done | bytes 1572896 | tf_op jit(solution)/shard_map/all_to_all | solution.py:142
  280.7 6.6 %all-to-all-start.7 = ((bf16[8,32,24,128]{3,2,0,1:T(8,128)(2,1)}), bf16[8,32,24,128]{3,2,0,1:T(8,128)(2,1)}, u32[]{:S(2)}, u32[]{:S(2)}) async-start(bf16[8,32,24,128]{3,2,0,1:T(8,128)(2,1)} %copy.81), calls=%async_computation.7 | async-start | bytes 3145728 | tf_op jit(solution)/shard_map/all_to_all | solution.py:149
  287.4 3.0 copy.83
  290.4 18.2 %all-to-all-done.7 = bf16[8,32,24,128]{3,2,0,1:T(8,128)(2,1)} async-done(((bf16[8,32,24,128]{3,2,0,1:T(8,128)(2,1)}), bf16[8,32,24,128]{3,2,0,1:T(8,128)(2,1)}, u32[]{:S(2)}, u32[]{:S(2)}) %all-to-all-start.7) | async-done | bytes 1572896 | tf_op jit(solution)/shard_map/all_to_all | solution.py:149
  308.6 6.6 %all-to-all-start.8 = ((bf16[8,32,24,128]{3,2,0,1:T(8,128)(2,1)}), bf16[8,32,24,128]{3,2,0,1:T(8,128)(2,1)}, u32[]{:S(2)}, u32[]{:S(2)}) async-start(bf16[8,32,24,128]{3,2,0,1:T(8,128)(2,1)} %copy.83), calls=%async_computation.8 | async-start | bytes 3145728 | tf_op jit(solution)/shard_map/all_to_all | solution.py:156
  316.8 19.6 %all-to-all-done.8 = bf16[8,32,24,128]{3,2,0,1:T(8,128)(2,1)} async-done(((bf16[8,32,24,128]{3,2,0,1:T(8,128)(2,1)}), bf16[8,32,24,128]{3,2,0,1:T(8,128)(2,1)}, u32[]{:S(2)}, u32[]{:S(2)}) %all-to-all-start.8) | async-done | bytes 1572896 | tf_op jit(solution)/shard_map/all_to_all | solution.py:156
  336.4 5.9 %all-to-all-start.4 = ((bf16[8,32,24,128]{3,2,0,1:T(8,128)(2,1)}), bf16[8,32,24,128]{3,2,0,1:T(8,128)(2,1)S(1)}, u32[]{:S(2)}, u32[]{:S(2)}) async-start(bf16[8,32,24,128]{3,2,0,1:T(8,128)(2,1)} %copy.75), calls=%async_computation.4 | async-start | bytes 3145728 | tf_op jit(solution)/shard_map/all_to_all | solution.py:127
  343.8 2.6 copy.86
  346.4 1.7 copy.82
  349.7 1.7 copy.84
  353.0 10.5 %all-to-all-done.4 = bf16[8,32,24,128]{3,2,0,1:T(8,128)(2,1)S(1)} async-done(((bf16[8,32,24,128]{3,2,0,1:T(8,128)(2,1)}), bf16[8,32,24,128]{3,2,0,1:T(8,128)(2,1)S(1)}, u32[]{:S(2)}, u32[]{:S(2)}) %all-to-all-start.4) | async-done | bytes 1572896 | tf_op jit(solution)/shard_map/all_to_all | solution.py:127
  365.3 8.6 %convert_bitcast_fusion = bf16[1024,4,512]{0,2,1:T(8,128)(2,1)S(1)} fusion(s32[4,1024]{1,0:T(4,128)S(1)} %fusion.91, bf16[4,1536,128]{1,2,0:T(8,128)(2,1)} %copy.88, bf16[4,1536,128]{1,2,0:T(8,128)(2,1)} %copy.87, bf16[4,1536,128]{1,2,0:T(8,128)(2,1)S(1)} %copy-done, bf16[4,1536,128]{1,2,0:T(8,128)(2,1)} %copy.85), kind=kOutput, calls=%fused_computation.85 | convolution fusion | flops 6476005376 | bytes 10502144 | tf_op jit(solution)/shard_map/hbt,hbf->thf/dot_general | solution.py:168
  375.4 2.3 copy.89
  (137 shorter events, 90.4 us)
Async XLA Ops:
  1.7 1.6 copy-start.6
  1.7 14.8 %copy-start.1 = (bf16[1024,512]{1,0:T(8,128)(2,1)S(1)}, bf16[1024,512]{1,0:T(8,128)(2,1)}, u32[]{:S(2)}) copy-start(bf16[1024,512]{1,0:T(8,128)(2,1)} %param.9) | copy-start | bytes 3145732
  8.3 28.2 %all-to-all-start = ((s32[32,1,192]{2,1,0:T(1,128)}), s32[32,1,192]{2,1,0:T(1,128)S(1)}, u32[]{:S(2)}, u32[]{:S(2)}) async-start(s32[32,1,192]{2,1,0:T(1,128)} %reshape.140), calls=%async_computation | async-start | bytes 65536 | tf_op jit(solution)/shard_map/all_to_all | solution.py:120
  17.0 1.2 copy-start.2
  18.8 1.3 copy-start.3
  20.7 1.3 copy-start.4
  22.5 1.3 copy-start.5
  36.5 28.4 %all-to-all-start.1 = ((bf16[8,32,24,128]{3,2,0,1:T(8,128)(2,1)}), bf16[8,32,24,128]{3,2,0,1:T(8,128)(2,1)S(1)}, u32[]{:S(2)}, u32[]{:S(2)}) async-start(bf16[8,32,24,128]{3,2,0,1:T(8,128)(2,1)} %copy.69), calls=%async_computation.1 | async-start | bytes 3145728 | tf_op jit(solution)/shard_map/all_to_all | solution.py:117
  64.9 27.8 %all-to-all-start.2 = ((bf16[8,32,24,128]{3,2,0,1:T(8,128)(2,1)}), bf16[8,32,24,128]{3,2,0,1:T(8,128)(2,1)}, u32[]{:S(2)}, u32[]{:S(2)}) async-start(bf16[8,32,24,128]{3,2,0,1:T(8,128)(2,1)} %copy.71), calls=%async_computation.2 | async-start | bytes 3145728 | tf_op jit(solution)/shard_map/all_to_all | solution.py:118
  92.7 27.8 %all-to-all-start.3 = ((bf16[8,32,24,128]{3,2,0,1:T(8,128)(2,1)}), bf16[8,32,24,128]{3,2,0,1:T(8,128)(2,1)}, u32[]{:S(2)}, u32[]{:S(2)}) async-start(bf16[8,32,24,128]{3,2,0,1:T(8,128)(2,1)} %copy.73), calls=%async_computation.3 | async-start | bytes 3145728 | tf_op jit(solution)/shard_map/all_to_all | solution.py:119
  120.6 39.5 %all-to-all-start.5 = ((bf16[8,32,24,128]{3,2,0,1:T(8,128)(2,1)}), bf16[8,32,24,128]{3,2,0,1:T(8,128)(2,1)S(1)}, u32[]{:S(2)}, u32[]{:S(2)}) async-start(bf16[8,32,24,128]{3,2,0,1:T(8,128)(2,1)} %copy.77), calls=%async_computation.5 | async-start | bytes 3145728 | tf_op jit(solution)/shard_map/all_to_all | solution.py:134
  252.2 28.5 %all-to-all-start.6 = ((bf16[8,32,24,128]{3,2,0,1:T(8,128)(2,1)}), bf16[8,32,24,128]{3,2,0,1:T(8,128)(2,1)S(1)}, u32[]{:S(2)}, u32[]{:S(2)}) async-start(bf16[8,32,24,128]{3,2,0,1:T(8,128)(2,1)} %copy.79), calls=%async_computation.6 | async-start | bytes 3145728 | tf_op jit(solution)/shard_map/all_to_all | solution.py:142
  280.7 27.8 %all-to-all-start.7 = ((bf16[8,32,24,128]{3,2,0,1:T(8,128)(2,1)}), bf16[8,32,24,128]{3,2,0,1:T(8,128)(2,1)}, u32[]{:S(2)}, u32[]{:S(2)}) async-start(bf16[8,32,24,128]{3,2,0,1:T(8,128)(2,1)} %copy.81), calls=%async_computation.7 | async-start | bytes 3145728 | tf_op jit(solution)/shard_map/all_to_all | solution.py:149
  308.6 27.8 %all-to-all-start.8 = ((bf16[8,32,24,128]{3,2,0,1:T(8,128)(2,1)}), bf16[8,32,24,128]{3,2,0,1:T(8,128)(2,1)}, u32[]{:S(2)}, u32[]{:S(2)}) async-start(bf16[8,32,24,128]{3,2,0,1:T(8,128)(2,1)} %copy.83), calls=%async_computation.8 | async-start | bytes 3145728 | tf_op jit(solution)/shard_map/all_to_all | solution.py:156
  336.4 27.1 %all-to-all-start.4 = ((bf16[8,32,24,128]{3,2,0,1:T(8,128)(2,1)}), bf16[8,32,24,128]{3,2,0,1:T(8,128)(2,1)S(1)}, u32[]{:S(2)}, u32[]{:S(2)}) async-start(bf16[8,32,24,128]{3,2,0,1:T(8,128)(2,1)} %copy.75), calls=%async_computation.4 | async-start | bytes 3145728 | tf_op jit(solution)/shard_map/all_to_all | solution.py:127
  363.7 1.6 copy-start
where the time goes:
time: 388 us; the launch traced here: 382 us
  matrix products  119 us (31%)
  waiting for transfers between devices  116 us (30%)
  local copies, waits for them, and re-layouts  62.7 us (16%)
  starting transfers between devices  61.4 us (16%)
  other arithmetic  20.9 us (5%)
    dot_general x16, matrix products, probabilities(): lax.dot_general(query_part, key_part, (((1,), (1,)), ((), ())), preferred...  28.5 us
    all_to_all x1, waiting for transfers between devices, on_device(): lax.all_to_all(owned_grads[2].reshape(groups, seq_count, slot_count, head...  19.6 us
    all_to_all x1, waiting for transfers between devices, on_device(): lax.all_to_all(owned_grads[1].reshape(groups, seq_count, slot_count, head...  18.2 us
    all_to_all x1, waiting for transfers between devices, on_device(): lax.all_to_all(key_buffer, 'seq', split_axis=1, concat_axis=1, tiled=True)  18.2 us
    all_to_all x1, waiting for transfers between devices, on_device(): lax.all_to_all(query_buffer, 'seq', split_axis=1, concat_axis=1, tiled=True)  18 us
    all_to_all x1, waiting for transfers between devices, on_device(): lax.all_to_all(owned_grads[0].reshape(groups, seq_count, slot_count, head...  18 us
    dot_general x8, matrix products, gradients(): lax.dot_general(coarse, upstream, (((0,), (0,)), ((), ())), preferred_ele...  17.1 us
    dot_general x8, matrix products, gradients(): lax.dot_general(slope, query_part, (((0,), (0,)), ((), ())), preferred_el...  16.7 us
  transfers between devices with their start and end apart: 9, of which 7 were waited for; matrix products, arithmetic and copies ran while one was open for 22% of the time, Pallas kernels for 0%

commit v1 on v0

v1 whole, which is shorter than its diff:
```python
import functools

import jax
import jax.numpy as jnp
from jax import lax
from jax.experimental import pallas as pl
from jax.experimental.pallas import tpu as pltpu
from jax.sharding import PartitionSpec as P

HEAD = 128
CLUSTERS = 64
SLOT = 24
BLOCK = 256
FIELDS = 4
TIGHT = 148
SORTED_ROUNDS = 2
VMEM = pltpu.CompilerParams(vmem_limit_bytes=60 * 1024 * 1024)
F32 = jnp.float32
BF16 = jnp.bfloat16
I32 = jnp.int32


def iota(shape, dim):
    return lax.broadcasted_iota(I32, shape, dim)


def against(a, b):
    return lax.dot_general(a, b, (((1,), (1,)), ((), ())), preferred_element_type=F32)


def across(a, b):
    return lax.dot_general(a, b, (((0,), (0,)), ((), ())), preferred_element_type=F32)


def smem():
    return pl.BlockSpec(memory_space=pltpu.SMEM)


def whole():
    return pl.BlockSpec(memory_space=pltpu.VMEM)


def pad_rows(capacity):
    return (capacity + SLOT + 7) // 8 * 8


def rank_kernel(ids_ref, pos_ref, count_ref, start_ref):
    heads, tokens = ids_ref.shape
    pairs = heads * CLUSTERS
    marks = jnp.concatenate(
        [
            (ids_ref[h : h + 1, :] == iota((CLUSTERS, tokens), 0)).astype(BF16)
            for h in range(heads)
        ],
        axis=0,
    )
    row, col = iota((pairs, pairs), 0), iota((pairs, pairs), 1)
    earlier = ((col < row) & (col // CLUSTERS == row // CLUSTERS)).astype(BF16)
    count_wide = against(marks, jnp.ones((128, tokens), BF16))
    start_wide = jnp.dot(earlier, count_wide.astype(BF16), preferred_element_type=F32)
    count_line = against(jnp.ones((8, tokens), BF16), marks)
    count_ref[...] = count_line.astype(I32)
    start_ref[...] = against(count_line.astype(BF16), earlier).astype(I32)
    upper = (iota((BLOCK, BLOCK), 0) < iota((BLOCK, BLOCK), 1)).astype(BF16)
    carry = start_wide[:, :1]
    for b in range(tokens // BLOCK):
        part = marks[:, b * BLOCK : (b + 1) * BLOCK]
        before = jnp.dot(part, upper, preferred_element_type=F32) + carry
        wide = part.astype(F32)
        carry = carry + jnp.sum(wide, axis=1, keepdims=True)
        place = wide * before
        for h in range(heads):
            pos_ref[h : h + 1, b * BLOCK : (b + 1) * BLOCK] = jnp.sum(
                place[h * CLUSTERS : (h + 1) * CLUSTERS], axis=0, keepdims=True
            ).astype(I32)


def sort_kernel(pos_ref, q_ref, k_ref, v_ref, g_ref, out_ref):
    tokens = q_ref.shape[0]
    where = pos_ref[pl.ds(pl.program_id(0), 1), :]
    fields = jnp.concatenate([q_ref[...], k_ref[...], v_ref[...], g_ref[...]], axis=1)
    for b in range(tokens // BLOCK):
        select = (where == iota((BLOCK, tokens), 0) + b * BLOCK).astype(BF16)
        rows = jnp.dot(select, fields, preferred_element_type=F32)
        for a in range(FIELDS):
            out_ref[a, b * BLOCK : (b + 1) * BLOCK, :] = rows[:, a * HEAD : (a + 1) * HEAD]


def plan_kernel(count_ref, list_ref, most_ref):
    owners, pairs = count_ref.shape
    rounds = pairs // owners
    counts = count_ref[...].astype(F32)
    row, col = iota((pairs, pairs), 0), iota((pairs, pairs), 1)
    total_line = jnp.sum(counts, axis=0, keepdims=True)
    total_col = jnp.sum(jnp.where(row == col, total_line, 0.0), axis=1, keepdims=True)
    ahead = (total_line > total_col) | ((total_line == total_col) & (col < row))
    rank_col = jnp.sum(ahead.astype(F32), axis=1, keepdims=True)
    at_rank = rank_col == col.astype(F32)
    order_line = jnp.sum(jnp.where(at_rank, row.astype(F32), 0.0), axis=0, keepdims=True)
    size_line = jnp.sum(jnp.where(at_rank, total_col, 0.0), axis=0, keepdims=True)
    device = iota((owners, 1), 0).astype(F32)
    lane = iota((owners, pairs), 1).astype(F32)
    near, far = iota((owners, owners), 0), iota((owners, owners), 1)
    load = jnp.zeros((owners, 1), F32)
    lists = jnp.zeros((owners, 128), F32)
    owned = jnp.zeros((owners, pairs), F32)
    for r in range(rounds):
        if r >= rounds - SORTED_ROUNDS:
            load_line = jnp.sum(jnp.where(near == far, load, 0.0), axis=0, keepdims=True)
            lighter = (load_line < load) | ((load_line == load) & (far < near))
            turn = jnp.sum(lighter.astype(F32), axis=1, keepdims=True)
        elif r % 2 == 0:
            turn = device
        else:
            turn = owners - 1.0 - device
        pick = lane == turn + float(r * owners)
        item = jnp.sum(jnp.where(pick, order_line, 0.0), axis=1, keepdims=True)
        load = load + jnp.sum(jnp.where(pick, size_line, 0.0), axis=1, keepdims=True)
        lists = jnp.where(iota((owners, 128), 1) == r, item, lists)
        owned = jnp.where(lane == item, 1.0, owned)
    list_ref[...] = lists.astype(I32)
    sent = against(counts.astype(BF16), owned.astype(BF16))
    most = jnp.max(jnp.max(sent, axis=1, keepdims=True), axis=0, keepdims=True)
    most_ref[...] = jnp.broadcast_to(most, most_ref.shape).astype(I32)


def pack_kernel(capacity, rounds, list_ref, count_ref, start_ref, sorted_ref, out_ref, table_ref, block):
    d = pl.program_id(0)
    tokens = (sorted_ref.shape[1] - 32) // (count_ref.shape[1] // CLUSTERS)
    padded = block.shape[1]
    offset = 0
    for j in range(rounds):
        item = list_ref[d, j]
        source = item // CLUSTERS * tokens + start_ref[0, item]
        for a in range(FIELDS):
            block[a, pl.ds(offset, SLOT), :] = sorted_ref[a, pl.ds(source, SLOT), :]
        table_ref[item] = d * padded + offset
        offset = offset + count_ref[0, item]
    for a in range(FIELDS):
        out_ref[0, a * capacity : (a + 1) * capacity, :] = block[a, :capacity, :].astype(BF16)


def attend_kernel(
    capacity, rounds, me_ref, list_ref, count_ref, in_ref, out_ref, arrived, leaving, gathered, work, done, used
):
    sources = in_ref.shape[0]
    most = work.shape[1]
    factor = float(HEAD) ** -0.5
    me = me_ref[0]

    def widen(s, _):
        used[s] = 0
        for a in range(FIELDS):
            arrived[s * FIELDS + a, :capacity, :] = in_ref[
                s, a * capacity : (a + 1) * capacity, :
            ].astype(F32)
        return 0

    lax.fori_loop(0, sources, widen, 0)

    def row_block(b):
        rows = slice(b * BLOCK, (b + 1) * BLOCK)
        width = (b + 1) * BLOCK
        query, upstream = work[0, rows, :], work[3, rows, :]
        keys, values = work[1, :width, :], work[2, :width, :]
        scores = against(query, keys) * factor
        allowed = iota((BLOCK, width), 1) <= iota((BLOCK, width), 0) + b * BLOCK
        scores = jnp.where(allowed, scores, -jnp.inf)
        weights = jnp.exp(scores - jnp.max(scores, axis=1, keepdims=True))
        shares = weights * (1.0 / jnp.sum(weights, axis=1, keepdims=True))
        coarse = shares.astype(BF16)
        attended = jnp.dot(coarse, values, preferred_element_type=F32)
        through = against(upstream, values)
        row_dot = jnp.sum(
            upstream.astype(F32) * attended.astype(BF16).astype(F32), axis=1, keepdims=True
        )
        slope = (shares * (through - row_dot)).astype(BF16)
        done[0, rows, :] = attended
        done[1, rows, :] = factor * jnp.dot(slope, keys, preferred_element_type=F32)
        key_grad = factor * across(slope, query)
        value_grad = across(coarse, upstream)
        if b > 0:
            old = slice(0, b * BLOCK)
            done[2, old, :] += key_grad[old]
            done[3, old, :] += value_grad[old]
        done[2, rows, :] = key_grad[rows]
        done[3, rows, :] = value_grad[rows]

    def one(j, _):
        item = list_ref[me, j]

        def collect(s, filled):
            for a in range(FIELDS):
                gathered[a, pl.ds(filled, SLOT), :] = arrived[
                    s * FIELDS + a, pl.ds(used[s], SLOT), :
                ]
            return filled + count_ref[s, item]

        total = lax.fori_loop(0, sources, collect, jnp.int32(0), unroll=4)
        for a in range(FIELDS):
            gathered[a, pl.ds(total, BLOCK), :] = jnp.zeros((BLOCK, HEAD), F32)
        for b in range(most // BLOCK):

            @pl.when(total > b * BLOCK)
            def _():
                rows = slice(b * BLOCK, (b + 1) * BLOCK)
                for a in range(FIELDS):
                    work[a, rows, :] = gathered[a, rows, :].astype(BF16)
                row_block(b)

        def deliver(s, filled):
            place = used[s]
            for a in range(FIELDS):
                leaving[s * FIELDS + a, pl.ds(place, SLOT), :] = done[
                    a, pl.ds(filled, SLOT), :
                ]
            used[s] = place + count_ref[s, item]
            return filled + count_ref[s, item]

        lax.fori_loop(0, sources, deliver, jnp.int32(0), unroll=4)
        return 0

    lax.fori_loop(0, rounds, one, 0)

    def narrow(s, _):
        for a in range(FIELDS):
            out_ref[s, a * capacity : (a + 1) * capacity, :] = leaving[
                s * FIELDS + a, :capacity, :
            ].astype(BF16)
        return 0

    lax.fori_loop(0, sources, narrow, 0)


def unpack_kernel(capacity, table_ref, start_ref, pos_ref, in_ref, o_ref, dq_ref, dk_ref, dv_ref, wide, rows):
    h = pl.program_id(0)
    owners = in_ref.shape[0]
    tokens = o_ref.shape[0]
    padded = pad_rows(capacity)

    @pl.when(h == 0)
    def _():
        def widen(d, _):
            for a in range(FIELDS):
                wide[a, pl.ds(pl.multiple_of(d * padded, 8), capacity), :] = in_ref[
                    d, a * capacity : (a + 1) * capacity, :
                ].astype(F32)
            return 0

        lax.fori_loop(0, owners, widen, 0)

    def put(c, _):
        item = h * CLUSTERS + c
        target = start_ref[0, item]
        source = table_ref[item]
        for a in range(FIELDS):
            rows[a, pl.ds(target, SLOT), :] = wide[a, pl.ds(source, SLOT), :]
        return 0

    lax.fori_loop(0, CLUSTERS, put, 0, unroll=4)
    fields = jnp.concatenate([rows[a, :tokens, :].astype(BF16) for a in range(FIELDS)], axis=1)
    lane = iota((tokens, 128), 1)
    place = jnp.sum(jnp.where(lane == h, pos_ref[...], 0), axis=1, keepdims=True)
    for b in range(tokens // BLOCK):
        part = slice(b * BLOCK, (b + 1) * BLOCK)
        select = (place[part] == iota((BLOCK, tokens), 1)).astype(BF16)
        result = jnp.dot(select, fields, preferred_element_type=F32).astype(BF16)
        for a, ref in enumerate((o_ref, dq_ref, dk_ref, dv_ref)):
            ref[part, :] = result[:, a * HEAD : (a + 1) * HEAD]


def on_device(queries, key_rows, value_rows, grad_out, cluster_ids):
    tokens, heads = cluster_ids.shape
    owners = lax.axis_size("seq")
    pairs = heads * CLUSTERS
    rounds = pairs // owners
    sorted_rows = heads * tokens + 32
    most = owners * SLOT
    me = lax.axis_index("seq").astype(I32).reshape(1)

    place, count, start = pl.pallas_call(
        rank_kernel,
        out_shape=(
            jax.ShapeDtypeStruct((heads, tokens), I32),
            jax.ShapeDtypeStruct((8, pairs), I32),
            jax.ShapeDtypeStruct((8, pairs), I32),
        ),
        in_specs=[whole()],
        out_specs=(whole(),) * 3,
        compiler_params=VMEM,
        name="rank",
    )(cluster_ids.T)

    every_count = lax.all_to_all(
        jnp.broadcast_to(count[:1], (owners, pairs)), "seq", 0, 0, tiled=True
    )

    field_spec = pl.BlockSpec((tokens, HEAD), lambda h: (0, h))
    in_order = pl.pallas_call(
        sort_kernel,
        grid=(heads,),
        out_shape=jax.ShapeDtypeStruct((FIELDS, sorted_rows, HEAD), F32),
        in_specs=[pl.BlockSpec((heads, tokens), lambda h: (0, 0))] + [field_spec] * 4,
        out_specs=pl.BlockSpec((FIELDS, tokens, HEAD), lambda h: (0, h, 0)),
        cost_estimate=pl.CostEstimate(
            flops=2 * heads * tokens * tokens * FIELDS * HEAD,
            bytes_accessed=6 * FIELDS * heads * tokens * HEAD,
            transcendentals=0,
        ),
        compiler_params=VMEM,
        name="sort",
    )(place, queries, key_rows, value_rows, grad_out)

    lists, heaviest = pl.pallas_call(
        plan_kernel,
        out_shape=(
            jax.ShapeDtypeStruct((owners, 128), I32),
            jax.ShapeDtypeStruct((8, 128), I32),
        ),
        in_specs=[whole()],
        out_specs=(whole(),) * 2,
        compiler_params=VMEM,
        name="plan",
    )(every_count)

    token_places = jnp.pad(place.T, ((0, 0), (0, 128 - heads)))

    def exchange(capacity):
        padded = pad_rows(capacity)
        packed = jax.ShapeDtypeStruct((owners, FIELDS * capacity, HEAD), BF16)
        block = pl.BlockSpec((1, FIELDS * capacity, HEAD), lambda d: (d, 0, 0))
        sending, table = pl.pallas_call(
            functools.partial(pack_kernel, capacity, rounds),
            grid=(owners,),
            out_shape=(packed, jax.ShapeDtypeStruct((pairs,), I32)),
            in_specs=[smem(), smem(), smem(), pl.BlockSpec((FIELDS, sorted_rows, HEAD), lambda d: (0, 0, 0))],
            out_specs=(block, smem()),
            scratch_shapes=[pltpu.VMEM((FIELDS, padded, HEAD), F32)],
            compiler_params=VMEM,
            name="pack",
        )(lists, count, start, in_order)
        owned = lax.all_to_all(sending, "seq", 0, 0, tiled=True)
        results = pl.pallas_call(
            functools.partial(attend_kernel, capacity, rounds),
            out_shape=packed,
            in_specs=[smem(), smem(), smem(), whole()],
            out_specs=whole(),
            scratch_shapes=[
                pltpu.VMEM((owners * FIELDS, padded, HEAD), F32),
                pltpu.VMEM((owners * FIELDS, padded, HEAD), F32),
                pltpu.VMEM((FIELDS, most + BLOCK + SLOT, HEAD), F32),
                pltpu.VMEM((FIELDS, most, HEAD), BF16),
                pltpu.VMEM((FIELDS, most + SLOT, HEAD), F32),
                pltpu.SMEM((owners,), I32),
            ],
            compiler_params=VMEM,
            name="attend",
        )(me, lists, every_count, owned)
        returned = lax.all_to_all(results, "seq", 0, 0, tiled=True)
        return pl.pallas_call(
            functools.partial(unpack_kernel, capacity),
            grid=(heads,),
            out_shape=(jax.ShapeDtypeStruct(queries.shape, BF16),) * 4,
            in_specs=[
                smem(),
                smem(),
                pl.BlockSpec((tokens, 128), lambda h: (0, 0)),
                pl.BlockSpec((owners, FIELDS * capacity, HEAD), lambda h: (0, 0, 0)),
            ],
            out_specs=(field_spec,) * 4,
            scratch_shapes=[
                pltpu.VMEM((FIELDS, owners * padded, HEAD), F32),
                pltpu.VMEM((FIELDS, tokens + SLOT, HEAD), F32),
            ],
            compiler_params=VMEM,
            name="unpack",
        )(table, start, token_places, returned)

    return lax.cond(
        heaviest[0, 0] <= TIGHT,
        lambda: exchange(TIGHT),
        lambda: exchange(rounds * SLOT),
    )


def solution(mesh):
    spec = P("seq", "head")
    return jax.shard_map(
        on_device, mesh=mesh, in_specs=(spec,) * 5, out_specs=(spec,) * 4, check_vma=False
    )
```

time: 388 us -> 216 us (0.56); the launches traced: 382 us -> 215 us
  matrix products: 119 us -> 0 us
  Pallas kernels: 0 us -> 68.9 us
  blocking collectives: 0 us -> 63.8 us
  local copies, waits for them, and re-layouts: 62.7 us -> 2.92 us
  waiting for transfers between devices: 116 us -> 64 us
  starting transfers between devices: 61.4 us -> 14 us
  other arithmetic: 20.9 us -> 0 us
    dot_general x59 -> x0, matrix products: 119 us -> none  [the longest x16 28.5 us: probabilities(): lax.dot_general(query_part, key_part, (((1,), (1,)), ((), ())), preferred...]
    pallas_call x0 -> x6, Pallas kernels: none -> 68.9 us  [the longest x1 29.8 us: exchange(): pl.pallas_call(functools.partial(attend_kernel, capacity, rounds), out_sh...]
    all_to_all x0 -> x1, blocking collectives: none -> 63.8 us  [exchange(): owned = lax.all_to_all(sending, 'seq', 0, 0, tiled=True)]
    all_to_all x9 -> x2, waiting for transfers between devices: 116 us -> 64 us  [the longest x1 64 us: exchange(): returned = lax.all_to_all(results, 'seq', 0, 0, tiled=True)]
    all_to_all x9 -> x2, starting transfers between devices: 61.4 us -> 14 us  [the longest x1 8.21 us: on_device(): lax.all_to_all(jnp.broadcast_to(count[:1], (owners, pairs)), 'seq', 0, 0,...]
    reshape x17 -> x0, local copies, waits for them, and re-layouts: 30.5 us -> none  [the longest x4 9.28 us: buffer_of(): arranged[:, :, index * head_size:(index + 1) * head_size]]
    reduce_sum x24 -> x0, other arithmetic: 14.7 us -> none  [the longest x8 8.83 us: gradients(): jnp.sum(upstream.astype(jnp.float32) * attended_part.astype(jnp.float32),...]
    all_to_all x10 -> x0, local copies, waits for them, and re-layouts: 14.2 us -> none  [the longest x1 2.84 us: on_device(): lax.all_to_all(key_buffer, 'seq', split_axis=1, concat_axis=1, tiled=True)]
  transfers between devices with their start and end apart: 9 -> 2, of which waited for: 7 -> 1; matrix products, arithmetic and copies ran while one was open for 22% -> 1% of each run, Pallas kernels for 0% -> 4%
where the time goes in v1:
time: 216 us; the launch traced here: 215 us
  Pallas kernels  68.9 us (32%)
  waiting for transfers between devices  64 us (30%)
  blocking collectives  63.8 us (30%)
  starting transfers between devices  14 us (6%)
  local copies, waits for them, and re-layouts  2.92 us (1%)
    all_to_all x1, waiting for transfers between devices, exchange(): returned = lax.all_to_all(results, 'seq', 0, 0, tiled=True)  64 us
    all_to_all x1, blocking collectives, exchange(): owned = lax.all_to_all(sending, 'seq', 0, 0, tiled=True)  63.8 us
    pallas_call x1, Pallas kernels, exchange(): pl.pallas_call(functools.partial(attend_kernel, capacity, rounds), out_sh...  29.8 us
    pallas_call x1, Pallas kernels, exchange(): pl.pallas_call(functools.partial(pack_kernel, capacity, rounds), grid=(ow...  16 us
    pallas_call x1, Pallas kernels, exchange(): pl.pallas_call(functools.partial(unpack_kernel, capacity), grid=(heads,),...  11.3 us
    pallas_call x1, Pallas kernels, on_device(): pl.pallas_call(sort_kernel, grid=(heads,), out_shape=jax.ShapeDtypeStruct...  8.43 us
    all_to_all x1, starting transfers between devices, on_device(): lax.all_to_all(jnp.broadcast_to(count[:1], (owners, pairs)), 'seq', 0, 0,...  8.21 us
    all_to_all x1, starting transfers between devices, exchange(): returned = lax.all_to_all(results, 'seq', 0, 0, tiled=True)  5.8 us
  transfers between devices with their start and end apart: 2, of which 1 were waited for; matrix products, arithmetic and copies ran while one was open for 1% of the time, Pallas kernels for 4%

profile of v1, /device:TPU:34, one launch (start us, length us, event | category | flops | bytes accessed | tf_op | source)
XLA Modules:
  0.0 214.9 jit_solution(17611032938364115492)
XLA Ops:
  0.6 1.9 rank.1
  2.5 0.6 broadcast_in_dim.2
  3.2 8.2 %all-to-all-start.4 = ((s32[32,1,256]{2,1,0:T(1,128)}), s32[32,1,256]{2,1,0:T(1,128)S(1)}, u32[]{:S(2)}, u32[]{:S(2)}) async-start(s32[32,1,256]{2,1,0:T(1,128)} %broadcast_in_dim.2), calls=%async_computation.4 | async-start | bytes 65536 | tf_op jit(solution)/shard_map/all_to_all | solution.py:294
  11.4 8.4 %sort.1 = f32[4,4128,128]{2,1,0:T(8,128)} custom-call(s32[4,1024]{1,0:T(4,128)S(1)} %get-tuple-element.59.pos_ref, bf16[1024,512]{1,0:T(8,128)(2,1)} %q_ref.1, bf16[1024,512]{1,0:T(8,128)(2,1)} %k_ref.1, bf16[1024,512]{1,0:T(8,128)(2,1)} %v_ref.1, bf16[1024,512]{1,0:T(8,128)(2,1)} %g_ref.1), custom_call_target="tpu_custom_call" | custom-call | flops 4294967296 | bytes 12582912 | tf_op jit(solution)/shard_map/sort/pallas_call | solution.py:299
  19.8 0.0 all-to-all-done.4
  19.8 1.5 plan.1
  21.3 1.2 slice.10
  23.1 191.8 %conditional.1 = ((bf16[1024,512]{1,0:T(8,128)(2,1)}, bf16[1024,512]{1,0:T(8,128)(2,1)}, bf16[1024,512]{1,0:T(8,128)(2,1)}, bf16[1024,512]{1,0:T(8,128)(2,1)})) conditional(s32[]{:T(128)} %bitcast.4, (s32[32,128]{1,0:T(8,128)S(1)}, s32[8,256]{1,0:T(8,128)S(1)}, s32[8,256]{1,0:T(8,128)S(1)}, f32[4,4128,128]{2,1,0:T(8,128)}, s32[]{:T(128)}, ...), branch_computations={%region_0.1_spmd, %region_1.2_spmd} | conditional | bytes 32030764 | solution.py:379
  23.2 16.0 %pack.3 = (bf16[32,592,128]{2,1,0:T(8,128)(2,1)}, s32[256]{0:T(256)}) custom-call(s32[32,128]{1,0:T(8,128)S(1)} %get-tuple-element.37.list_ref, s32[8,256]{1,0:T(8,128)S(1)} %get-tuple-element.38.count_ref, s32[8,256]{1,0:T(8,128)S(1)} %get-tuple-element.39.start_ref, f32[4,4128,128]{2,1,0:T(8,128)} %get-tuple-element.40.sorted_ref), custom_call_target="tpu_custom_call" | custom-call | tf_op jit(solution)/shard_map/cond/branch_1_fun/pack/pallas_call | solution.py:332
  39.1 63.8 %all_to_all.25.in_ref = bf16[32,592,128]{2,1,0:T(8,128)(2,1)} all-to-all(bf16[32,592,128]{2,1,0:T(8,128)(2,1)} %get-tuple-element.45), channel_id=1, replica_groups=mesh['seq'=32,'head'=4] {'seq'}, dimensions={0} | all-to-all | bytes 9699328 | tf_op jit(solution)/shard_map/cond/branch_1_fun/all_to_all | solution.py:342
  103.0 29.8 %attend.3 = bf16[32,592,128]{2,1,0:T(8,128)(2,1)} custom-call(s32[1]{0:T(128)} %bitcast.1.me_ref, s32[32,128]{1,0:T(8,128)S(1)} %get-tuple-element.37.list_ref, s32[32,256]{1,0:T(8,128)S(1)} %get-tuple-element.44.count_ref, bf16[32,592,128]{2,1,0:T(8,128)(2,1)} %all_to_all.25.in_ref), custom_call_target="tpu_custom_call" | custom-call | tf_op jit(solution)/shard_map/cond/branch_1_fun/attend/pallas_call | solution.py:343
  132.8 5.8 %all-to-all-start.3 = ((bf16[32,592,128]{2,1,0:T(8,128)(2,1)}), bf16[32,592,128]{2,1,0:T(8,128)(2,1)}, u32[]{:S(2)}, u32[]{:S(2)}) async-start(bf16[32,592,128]{2,1,0:T(8,128)(2,1)} %attend.3), calls=%async_computation.3 | async-start | bytes 9699328 | tf_op jit(solution)/shard_map/cond/branch_1_fun/all_to_all | solution.py:359
  138.6 0.2 copy.20
  138.8 0.9 pad.6.pos_ref
  139.7 64.0 %all-to-all-done.3.in_ref = bf16[32,592,128]{2,1,0:T(8,128)(2,1)} async-done(((bf16[32,592,128]{2,1,0:T(8,128)(2,1)}), bf16[32,592,128]{2,1,0:T(8,128)(2,1)}, u32[]{:S(2)}, u32[]{:S(2)}) %all-to-all-start.3) | async-done | bytes 4849696 | tf_op jit(solution)/shard_map/cond/branch_1_fun/all_to_all | solution.py:359
  203.6 11.3 %unpack.3 = (bf16[1024,512]{1,0:T(8,128)(2,1)}, bf16[1024,512]{1,0:T(8,128)(2,1)}, bf16[1024,512]{1,0:T(8,128)(2,1)}, bf16[1024,512]{1,0:T(8,128)(2,1)}) custom-call(s32[256]{0:T(256)} %get-tuple-element.41.table_ref, s32[8,256]{1,0:T(8,128)S(1)} %get-tuple-element.39.start_ref, s32[1024,128]{1,0:T(8,128)} %pad.6.pos_ref, ...), custom_call_target="tpu_custom_call" | custom-call | tf_op jit(solution)/shard_map/cond/branch_1_fun/unpack/pallas_call | solution.py:360
  (2 shorter events, 0.0 us)
Async XLA Ops:
  3.2 16.7 %all-to-all-start.4 = ((s32[32,1,256]{2,1,0:T(1,128)}), s32[32,1,256]{2,1,0:T(1,128)S(1)}, u32[]{:S(2)}, u32[]{:S(2)}) async-start(s32[32,1,256]{2,1,0:T(1,128)} %broadcast_in_dim.2), calls=%async_computation.4 | async-start | bytes 65536 | tf_op jit(solution)/shard_map/all_to_all | solution.py:294
  132.8 70.9 %all-to-all-start.3 = ((bf16[32,592,128]{2,1,0:T(8,128)(2,1)}), bf16[32,592,128]{2,1,0:T(8,128)(2,1)}, u32[]{:S(2)}, u32[]{:S(2)}) async-start(bf16[32,592,128]{2,1,0:T(8,128)(2,1)} %attend.3), calls=%async_computation.3 | async-start | bytes 9699328 | tf_op jit(solution)/shard_map/cond/branch_1_fun/all_to_all | solution.py:359

commit v2 on v1

--- a/solution.py
+++ b/solution.py
@@ -12,9 +12,10 @@
 SLOT = 24
 BLOCK = 256
 FIELDS = 4
-TIGHT = 148
-SORTED_ROUNDS = 2
-VMEM = pltpu.CompilerParams(vmem_limit_bytes=60 * 1024 * 1024)
+TIGHT = 144
+DEALS = ((0, 0, 0, 0, 0, 0), (27, 20, 16, 8, 9, 1), (2, 0, 5, 26, 20, 29), (11, 30, 23, 3, 17, 6))
+OWNERS_AT_ONCE = 8
+LOG2_E = 1.4426950408889634
 F32 = jnp.float32
 BF16 = jnp.bfloat16
 I32 = jnp.int32
@@ -30,6 +31,10 @@
 
 def across(a, b):
     return lax.dot_general(a, b, (((0,), (0,)), ((), ())), preferred_element_type=F32)
+
+
+def limit(mib):
+    return pltpu.CompilerParams(vmem_limit_bytes=mib * 1024 * 1024)
 
 
 def smem():
@@ -58,9 +63,9 @@
     earlier = ((col < row) & (col // CLUSTERS == row // CLUSTERS)).astype(BF16)
     count_wide = against(marks, jnp.ones((128, tokens), BF16))
     start_wide = jnp.dot(earlier, count_wide.astype(BF16), preferred_element_type=F32)
-    count_line = against(jnp.ones((8, tokens), BF16), marks)
+    count_line = against(jnp.ones((count_ref.shape[0], tokens), BF16), marks)
     count_ref[...] = count_line.astype(I32)
-    start_ref[...] = against(count_line.astype(BF16), earlier).astype(I32)
+    start_ref[...] = against(count_line[:8].astype(BF16), earlier).astype(I32)
     upper = (iota((BLOCK, BLOCK), 0) < iota((BLOCK, BLOCK), 1)).astype(BF16)
     carry = start_wide[:, :1]
     for b in range(tokens // BLOCK):
@@ -83,12 +88,15 @@
         select = (where == iota((BLOCK, tokens), 0) + b * BLOCK).astype(BF16)
         rows = jnp.dot(select, fields, preferred_element_type=F32)
         for a in range(FIELDS):
-            out_ref[a, b * BLOCK : (b + 1) * BLOCK, :] = rows[:, a * HEAD : (a + 1) * HEAD]
+            out_ref[0, a, b * BLOCK : (b + 1) * BLOCK, :] = rows[
+                :, a * HEAD : (a + 1) * HEAD
+            ].astype(BF16)
 
 
 def plan_kernel(count_ref, list_ref, most_ref):
     owners, pairs = count_ref.shape
     rounds = pairs // owners
+    deals = len(DEALS)
     counts = count_ref[...].astype(F32)
     row, col = iota((pairs, pairs), 0), iota((pairs, pairs), 1)
     total_line = jnp.sum(counts, axis=0, keepdims=True)
@@ -98,46 +106,81 @@
     at_rank = rank_col == col.astype(F32)
     order_line = jnp.sum(jnp.where(at_rank, row.astype(F32), 0.0), axis=0, keepdims=True)
     size_line = jnp.sum(jnp.where(at_rank, total_col, 0.0), axis=0, keepdims=True)
-    device = iota((owners, 1), 0).astype(F32)
-    lane = iota((owners, pairs), 1).astype(F32)
-    near, far = iota((owners, owners), 0), iota((owners, owners), 1)
-    load = jnp.zeros((owners, 1), F32)
-    lists = jnp.zeros((owners, 128), F32)
-    owned = jnp.zeros((owners, pairs), F32)
+    seats = deals * owners
+    seat = iota((seats, 1), 0)
+    device, deal = seat % owners, seat // owners
+    lane = iota((seats, pairs), 1).astype(F32)
+    near, far = iota((seats, seats), 0), iota((seats, seats), 1)
+    together = near // owners == far // owners
+    load = jnp.zeros((seats, 1), F32)
+    lists = jnp.zeros((seats, 128), F32)
+    owned = jnp.zeros((seats, pairs), F32)
     for r in range(rounds):
-        if r >= rounds - SORTED_ROUNDS:
+        if r >= len(DEALS[0]):
             load_line = jnp.sum(jnp.where(near == far, load, 0.0), axis=0, keepdims=True)
             lighter = (load_line < load) | ((load_line == load) & (far < near))
-            turn = jnp.sum(lighter.astype(F32), axis=1, keepdims=True)
-        elif r % 2 == 0:
-            turn = device
+            turn = jnp.sum((lighter & together).astype(F32), axis=1, keepdims=True)
         else:
-            turn = owners - 1.0 - device
+            shift = jnp.zeros((seats, 1), I32)
+            for c in range(deals):
+                shift = jnp.where(deal == c, DEALS[c][r], shift)
+            turn = (device + shift) % owners
+            if r % 2 == 1:
+                turn = owners - 1 - turn
+            turn = turn.astype(F32)
         pick = lane == turn + float(r * owners)
         item = jnp.sum(jnp.where(pick, order_line, 0.0), axis=1, keepdims=True)
         load = load + jnp.sum(jnp.where(pick, size_line, 0.0), axis=1, keepdims=True)
-        lists = jnp.where(iota((owners, 128), 1) == r, item, lists)
+        lists = jnp.where(iota((seats, 128), 1) == r, item, lists)
         owned = jnp.where(lane == item, 1.0, owned)
-    list_ref[...] = lists.astype(I32)
     sent = against(counts.astype(BF16), owned.astype(BF16))
-    most = jnp.max(jnp.max(sent, axis=1, keepdims=True), axis=0, keepdims=True)
-    most_ref[...] = jnp.broadcast_to(most, most_ref.shape).astype(I32)
-
-
-def pack_kernel(capacity, rounds, list_ref, count_ref, start_ref, sorted_ref, out_ref, table_ref, block):
-    d = pl.program_id(0)
-    tokens = (sorted_ref.shape[1] - 32) // (count_ref.shape[1] // CLUSTERS)
-    padded = block.shape[1]
-    offset = 0
-    for j in range(rounds):
-        item = list_ref[d, j]
-        source = item // CLUSTERS * tokens + start_ref[0, item]
-        for a in range(FIELDS):
-            block[a, pl.ds(offset, SLOT), :] = sorted_ref[a, pl.ds(source, SLOT), :]
-        table_ref[item] = d * padded + offset
-        offset = offset + count_ref[0, item]
-    for a in range(FIELDS):
-        out_ref[0, a * capacity : (a + 1) * capacity, :] = block[a, :capacity, :].astype(BF16)
+    heaviest = jnp.max(sent, axis=0, keepdims=True)
+    seat_line = iota((1, seats), 1)
+    least = None
+    for c in range(deals):
+        most = jnp.max(
+            jnp.where(seat_line // owners == c, heaviest, 0.0), axis=1, keepdims=True
+        )
+        mine = lists[c * owners : (c + 1) * owners]
+        if least is None:
+            least, chosen = most, mine
+        else:
+            chosen = jnp.where(most < least, mine, chosen)
+            least = jnp.minimum(least, most)
+    list_ref[...] = chosen.astype(I32)
+    most_ref[...] = jnp.broadcast_to(least, most_ref.shape).astype(I32)
+
+
+def pack_kernel(
+    capacity, rounds, heads, list_ref, count_ref, start_ref, sorted_ref, out_ref, table_ref, rows, block
+):
+    step = pl.program_id(0)
+    tokens = sorted_ref.shape[2]
+    padded = block.shape[2]
+
+    @pl.when(step < heads)
+    def _():
+        place = pl.multiple_of(step * tokens, 8)
+        for a in range(FIELDS):
+            rows[a, pl.ds(place, tokens), :] = sorted_ref[0, a].astype(F32)
+
+    @pl.when(step >= heads)
+    def _():
+        for o in range(OWNERS_AT_ONCE):
+            d = (step - heads) * OWNERS_AT_ONCE + o
+            items = [list_ref[d, j] for j in range(rounds)]
+            counts = [count_ref[0, item] for item in items]
+            sources = [item // CLUSTERS * tokens + start_ref[0, item] for item in items]
+            offset = 0
+            for j in range(rounds):
+                for a in range(FIELDS):
+                    block[o, a, pl.ds(offset, SLOT), :] = rows[a, pl.ds(sources[j], SLOT), :]
+                table_ref[items[j]] = d * padded + offset
+                offset = offset + counts[j]
+            for a in range(FIELDS):
+                out_ref[o, a * capacity : (a + 1) * capacity, :] = block[
+                    o, a, :capacity, :
+                ].astype(BF16)
 
 
 def attend_kernel(
@@ -158,33 +201,38 @@
 
     lax.fori_loop(0, sources, widen, 0)
 
-    def row_block(b):
-        rows = slice(b * BLOCK, (b + 1) * BLOCK)
-        width = (b + 1) * BLOCK
-        query, upstream = work[0, rows, :], work[3, rows, :]
-        keys, values = work[1, :width, :], work[2, :width, :]
-        scores = against(query, keys) * factor
-        allowed = iota((BLOCK, width), 1) <= iota((BLOCK, width), 0) + b * BLOCK
-        scores = jnp.where(allowed, scores, -jnp.inf)
-        weights = jnp.exp(scores - jnp.max(scores, axis=1, keepdims=True))
-        shares = weights * (1.0 / jnp.sum(weights, axis=1, keepdims=True))
-        coarse = shares.astype(BF16)
-        attended = jnp.dot(coarse, values, preferred_element_type=F32)
-        through = against(upstream, values)
-        row_dot = jnp.sum(
-            upstream.astype(F32) * attended.astype(BF16).astype(F32), axis=1, keepdims=True
-        )
-        slope = (shares * (through - row_dot)).astype(BF16)
-        done[0, rows, :] = attended
-        done[1, rows, :] = factor * jnp.dot(slope, keys, preferred_element_type=F32)
-        key_grad = factor * across(slope, query)
-        value_grad = across(coarse, upstream)
-        if b > 0:
-            old = slice(0, b * BLOCK)
-            done[2, old, :] += key_grad[old]
-            done[3, old, :] += value_grad[old]
-        done[2, rows, :] = key_grad[rows]
-        done[3, rows, :] = value_grad[rows]
+    def cluster(n):
+        size = n * BLOCK
+        query, keys, values, upstream = (work[a, :size, :] for a in range(FIELDS))
+        scale = factor * LOG2_E
+        below = iota((BLOCK, BLOCK), 0) <= iota((BLOCK, BLOCK), 1)
+        keys_t = gathered[1, :size, :].T.astype(BF16)
+        values_t = gathered[2, :size, :].T.astype(BF16)
+        up_t = gathered[3, :size, :].T
+        cols = [slice(b * BLOCK, (b + 1) * BLOCK) for b in range(n)]
+        scores = [against(keys[: (b + 1) * BLOCK], query[cols[b]]) for b in range(n)]
+        through = [against(values[: (b + 1) * BLOCK], upstream[cols[b]]) for b in range(n)]
+        coarse = []
+        slope = []
+        for b in range(n):
+            s = scores[b]
+            last = jnp.where(below, s[b * BLOCK :], -jnp.inf)
+            s = last if b == 0 else jnp.concatenate([s[: b * BLOCK], last], axis=0)
+            weights = jnp.exp2((s - jnp.max(s, axis=0, keepdims=True)) * scale)
+            shares = weights * (1.0 / jnp.sum(weights, axis=0, keepdims=True))
+            rough = shares.astype(BF16)
+            attended = jnp.dot(values_t[:, : (b + 1) * BLOCK], rough, preferred_element_type=F32)
+            done[0, cols[b], :] = attended.T
+            row_dot = jnp.sum(up_t[:, cols[b]] * attended.astype(BF16).astype(F32), axis=0, keepdims=True)
+            bend = (shares * (through[b] - row_dot)).astype(BF16)
+            done[1, cols[b], :] = factor * jnp.dot(keys_t[:, : (b + 1) * BLOCK], bend, preferred_element_type=F32).T
+            coarse.append(rough)
+            slope.append(bend)
+        for k in range(n):
+            c = jnp.concatenate([x[cols[k]] for x in coarse[k:]], axis=1)
+            done[3, cols[k], :] = jnp.dot(c, upstream[k * BLOCK :], preferred_element_type=F32)
+            c = jnp.concatenate([x[cols[k]] for x in slope[k:]], axis=1)
+            done[2, cols[k], :] = factor * jnp.dot(c, query[k * BLOCK :], preferred_element_type=F32)
 
     def one(j, _):
         item = list_ref[me, j]
@@ -199,14 +247,17 @@
         total = lax.fori_loop(0, sources, collect, jnp.int32(0), unroll=4)
         for a in range(FIELDS):
             gathered[a, pl.ds(total, BLOCK), :] = jnp.zeros((BLOCK, HEAD), F32)
-        for b in range(most // BLOCK):
-
-            @pl.when(total > b * BLOCK)
+        blocks = most // BLOCK
+        for n in range(1, blocks + 1):
+            enough = total > (n - 1) * BLOCK
+            if n < blocks:
+                enough = enough & (total <= n * BLOCK)
+
+            @pl.when(enough)
             def _():
-                rows = slice(b * BLOCK, (b + 1) * BLOCK)
                 for a in range(FIELDS):
-                    work[a, rows, :] = gathered[a, rows, :].astype(BF16)
-                row_block(b)
+                    work[a, : n * BLOCK, :] = gathered[a, : n * BLOCK, :].astype(BF16)
+                cluster(n)
 
         def deliver(s, filled):
             place = used[s]
@@ -274,7 +325,7 @@
     owners = lax.axis_size("seq")
     pairs = heads * CLUSTERS
     rounds = pairs // owners
-    sorted_rows = heads * tokens + 32
+    sorted_rows = heads * tokens + SLOT
     most = owners * SLOT
     me = lax.axis_index("seq").astype(I32).reshape(1)
 
@@ -282,32 +333,30 @@
         rank_kernel,
         out_shape=(
             jax.ShapeDtypeStruct((heads, tokens), I32),
-            jax.ShapeDtypeStruct((8, pairs), I32),
+            jax.ShapeDtypeStruct((owners, pairs), I32),
             jax.ShapeDtypeStruct((8, pairs), I32),
         ),
         in_specs=[whole()],
         out_specs=(whole(),) * 3,
-        compiler_params=VMEM,
+        compiler_params=limit(16),
         name="rank",
     )(cluster_ids.T)
 
-    every_count = lax.all_to_all(
-        jnp.broadcast_to(count[:1], (owners, pairs)), "seq", 0, 0, tiled=True
-    )
+    every_count = lax.all_to_all(count, "seq", 0, 0, tiled=True)
 
     field_spec = pl.BlockSpec((tokens, HEAD), lambda h: (0, h))
     in_order = pl.pallas_call(
         sort_kernel,
         grid=(heads,),
-        out_shape=jax.ShapeDtypeStruct((FIELDS, sorted_rows, HEAD), F32),
+        out_shape=jax.ShapeDtypeStruct((heads, FIELDS, tokens, HEAD), BF16),
         in_specs=[pl.BlockSpec((heads, tokens), lambda h: (0, 0))] + [field_spec] * 4,
-        out_specs=pl.BlockSpec((FIELDS, tokens, HEAD), lambda h: (0, h, 0)),
+        out_specs=pl.BlockSpec((1, FIELDS, tokens, HEAD), lambda h: (h, 0, 0, 0)),
         cost_estimate=pl.CostEstimate(
             flops=2 * heads * tokens * tokens * FIELDS * HEAD,
-            bytes_accessed=6 * FIELDS * heads * tokens * HEAD,
+            bytes_accessed=4 * FIELDS * heads * tokens * HEAD,
             transcendentals=0,
         ),
-        compiler_params=VMEM,
+        compiler_params=limit(16),
         name="sort",
     )(place, queries, key_rows, value_rows, grad_out)
 
@@ -319,7 +368,7 @@
         ),
         in_specs=[whole()],
         out_specs=(whole(),) * 2,
-        compiler_params=VMEM,
+        compiler_params=limit(16),
         name="plan",
     )(every_count)
 
@@ -328,15 +377,30 @@
     def exchange(capacity):
         padded = pad_rows(capacity)
         packed = jax.ShapeDtypeStruct((owners, FIELDS * capacity, HEAD), BF16)
-        block = pl.BlockSpec((1, FIELDS * capacity, HEAD), lambda d: (d, 0, 0))
         sending, table = pl.pallas_call(
-            functools.partial(pack_kernel, capacity, rounds),
-            grid=(owners,),
+            functools.partial(pack_kernel, capacity, rounds, heads),
+            grid=(heads + owners // OWNERS_AT_ONCE,),
             out_shape=(packed, jax.ShapeDtypeStruct((pairs,), I32)),
-            in_specs=[smem(), smem(), smem(), pl.BlockSpec((FIELDS, sorted_rows, HEAD), lambda d: (0, 0, 0))],
-            out_specs=(block, smem()),
-            scratch_shapes=[pltpu.VMEM((FIELDS, padded, HEAD), F32)],
-            compiler_params=VMEM,
+            in_specs=[
+                smem(),
+                smem(),
+                smem(),
+                pl.BlockSpec(
+                    (1, FIELDS, tokens, HEAD), lambda i: (jnp.minimum(i, heads - 1), 0, 0, 0)
+                ),
+            ],
+            out_specs=(
+                pl.BlockSpec(
+                    (OWNERS_AT_ONCE, FIELDS * capacity, HEAD),
+                    lambda i: (jnp.maximum(i - heads, 0), 0, 0),
+                ),
+                smem(),
+            ),
+            scratch_shapes=[
+                pltpu.VMEM((FIELDS, sorted_rows, HEAD), F32),
+                pltpu.VMEM((OWNERS_AT_ONCE, FIELDS, padded, HEAD), F32),
+            ],
+            compiler_params=limit(24),
             name="pack",
         )(lists, count, start, in_order)
         owned = lax.all_to_all(sending, "seq", 0, 0, tiled=True)
@@ -353,7 +417,7 @@
                 pltpu.VMEM((FIELDS, most + SLOT, HEAD), F32),
                 pltpu.SMEM((owners,), I32),
             ],
-            compiler_params=VMEM,
+            compiler_params=limit(48),
             name="attend",
         )(me, lists, every_count, owned)
         returned = lax.all_to_all(results, "seq", 0, 0, tiled=True)
@@ -372,7 +436,7 @@
                 pltpu.VMEM((FIELDS, owners * padded, HEAD), F32),
                 pltpu.VMEM((FIELDS, tokens + SLOT, HEAD), F32),
             ],
-            compiler_params=VMEM,
+            compiler_params=limit(36),
             name="unpack",
         )(table, start, token_places, returned)
 

time: 216 us -> 198 us (0.917)
  Pallas kernels: 68.9 us -> 46.8 us
  local copies, waits for them, and re-layouts: 2.92 us -> 9.2 us
    pallas_call x1, Pallas kernels: 29.8 us -> 20.1 us  [exchange(): pl.pallas_call(functools.partial(attend_kernel, capacity, rounds), out_sh...]
    pallas_call x1, Pallas kernels: 16 us -> 6.68 us  [exchange(): pl.pallas_call(functools.partial(pack_kernel, capacity, rounds, heads), g...]
    unnamed x1 -> x11, local copies, waits for them, and re-layouts: 0.01 us -> 5.61 us
  transfers between devices with their start and end apart: 2 -> 2, of which waited for: 1 -> 1; matrix products, arithmetic and copies ran while one was open for 1% -> 0% of each run, Pallas kernels for 4% -> 3%
where the time goes in v2:
time: 198 us; the launch traced here: 197 us
  waiting for transfers between devices  62.9 us (32%)
  blocking collectives  62.3 us (31%)
  Pallas kernels  46.8 us (24%)
  starting transfers between devices  13.9 us (7%)
  local copies, waits for them, and re-layouts  9.2 us (5%)
    all_to_all x1, waiting for transfers between devices, exchange(): returned = lax.all_to_all(results, 'seq', 0, 0, tiled=True)  62.9 us
    all_to_all x1, blocking collectives, exchange(): owned = lax.all_to_all(sending, 'seq', 0, 0, tiled=True)  62.3 us
    pallas_call x1, Pallas kernels, exchange(): pl.pallas_call(functools.partial(attend_kernel, capacity, rounds), out_sh...  20.1 us
    pallas_call x1, Pallas kernels, exchange(): pl.pallas_call(functools.partial(unpack_kernel, capacity), grid=(heads,),...  11 us
    all_to_all x1, starting transfers between devices, on_device(): every_count = lax.all_to_all(count, 'seq', 0, 0, tiled=True)  8.2 us
    pallas_call x1, Pallas kernels, on_device(): pl.pallas_call(sort_kernel, grid=(heads,), out_shape=jax.ShapeDtypeStruct...  6.8 us
    pallas_call x1, Pallas kernels, exchange(): pl.pallas_call(functools.partial(pack_kernel, capacity, rounds, heads), g...  6.68 us
    all_to_all x1, starting transfers between devices, exchange(): returned = lax.all_to_all(results, 'seq', 0, 0, tiled=True)  5.73 us
  transfers between devices with their start and end apart: 2, of which 1 were waited for; matrix products, arithmetic and copies ran while one was open for 0% of the time, Pallas kernels for 3%

profile of v2, /device:TPU:34, one launch (start us, length us, event | category | flops | bytes accessed | tf_op | source)
XLA Modules:
  0.0 196.6 jit_solution(3600627289254939273)
XLA Ops:
  0.6 0.0 copy-start.1
  0.6 0.7 copy-done.1
  1.3 1.2 rank.1
  2.5 0.6 copy.19
  3.2 8.2 %all-to-all-start.4 = ((s32[32,1,256]{2,1,0:T(1,128)}), s32[32,1,256]{2,1,0:T(1,128)S(1)}, u32[]{:S(2)}, u32[]{:S(2)}) async-start(s32[32,1,256]{2,1,0:T(1,128)} %copy.19), calls=%async_computation.4 | async-start | bytes 65536 | tf_op jit(solution)/shard_map/all_to_all | solution.py:345
  11.4 0.0 copy-start.2
  11.4 1.2 copy-done.2
  12.6 0.0 copy-start.3
  12.6 1.2 copy-done.3
  13.8 0.0 copy-start.4
  13.8 1.2 copy-done.4
  15.1 0.0 copy-start.5
  15.1 1.2 copy-done.5
  16.3 6.8 %sort.1 = bf16[4,4,1024,128]{3,2,1,0:T(8,128)(2,1)} custom-call(s32[4,1024]{1,0:T(4,128)S(1)} %get-tuple-element.59.pos_ref, bf16[1024,512]{1,0:T(8,128)(2,1)S(1)} %copy-done.2, bf16[1024,512]{1,0:T(8,128)(2,1)S(1)} %copy-done.3, bf16[1024,512]{1,0:T(8,128)(2,1)S(1)} %copy-done.4, bf16[1024,512]{1,0:T(8,128)(2,1)S(1)} %copy-done.5), custom_call_target="tpu_custom_call" | custom-call | flops 4294967296 | bytes 8388608 | tf_op jit(solution)/shard_map/sort/pallas_call | solution.py:348
  23.1 0.0 all-to-all-done.4
  23.1 1.1 plan.1
  24.2 0.5 slice.3
  25.3 171.3 %conditional.1 = ((bf16[1024,512]{1,0:T(8,128)(2,1)}, bf16[1024,512]{1,0:T(8,128)(2,1)}, bf16[1024,512]{1,0:T(8,128)(2,1)}, bf16[1024,512]{1,0:T(8,128)(2,1)})) conditional(s32[]{:T(128)} %bitcast.4, (s32[32,128]{1,0:T(8,128)S(1)}, s32[32,256]{1,0:T(8,128)S(1)}, s32[8,256]{1,0:T(8,128)S(1)}, bf16[4,4,1024,128]{3,2,1,0:T(8,128)(2,1)}, s32[]{:T(128)}, ...), branch_computations={%region_0.1_spmd, %region_1.2_spmd} | conditional | bytes 43040840 | solution.py:443
  25.4 6.7 %pack.3 = (bf16[32,576,128]{2,1,0:T(8,128)(2,1)S(1)}, s32[256]{0:T(256)S(1)}) custom-call(s32[32,128]{1,0:T(8,128)S(1)} %get-tuple-element.37.list_ref, s32[32,256]{1,0:T(8,128)S(1)} %get-tuple-element.38.count_ref, s32[8,256]{1,0:T(8,128)S(1)} %get-tuple-element.39.start_ref, bf16[4,4,1024,128]{3,2,1,0:T(8,128)(2,1)} %get-tuple-element.40.sorted_ref), custom_call_target="tpu_custom_call" | custom-call | tf_op jit(solution)/shard_map/cond/branch_1_fun/pack/pallas_call | solution.py:380
  32.0 62.3 %all_to_all.28.in_ref = bf16[32,576,128]{2,1,0:T(8,128)(2,1)} all-to-all(bf16[32,576,128]{2,1,0:T(8,128)(2,1)S(1)} %get-tuple-element.45), channel_id=1, replica_groups=mesh['seq'=32,'head'=4] {'seq'}, dimensions={0} | all-to-all | bytes 9437184 | tf_op jit(solution)/shard_map/cond/branch_1_fun/all_to_all | solution.py:406
  94.4 20.1 %attend.3 = bf16[32,576,128]{2,1,0:T(8,128)(2,1)S(1)} custom-call(s32[1]{0:T(128)} %bitcast.1.me_ref, s32[32,128]{1,0:T(8,128)S(1)} %get-tuple-element.37.list_ref, s32[32,256]{1,0:T(8,128)S(1)} %get-tuple-element.44.count_ref, bf16[32,576,128]{2,1,0:T(8,128)(2,1)} %all_to_all.28.in_ref), custom_call_target="tpu_custom_call" | custom-call | tf_op jit(solution)/shard_map/cond/branch_1_fun/attend/pallas_call | solution.py:407
  114.5 0.0 copy-start
  114.5 2.2 %copy-done = bf16[32,576,128]{2,1,0:T(8,128)(2,1)} copy-done((bf16[32,576,128]{2,1,0:T(8,128)(2,1)}, bf16[32,576,128]{2,1,0:T(8,128)(2,1)S(1)}, u32[]{:S(2)}) %copy-start) | copy-done | bytes 4718616 | tf_op jit(solution)/shard_map/cond
  116.6 5.7 %all-to-all-start.3 = ((bf16[32,576,128]{2,1,0:T(8,128)(2,1)}), bf16[32,576,128]{2,1,0:T(8,128)(2,1)}, u32[]{:S(2)}, u32[]{:S(2)}) async-start(bf16[32,576,128]{2,1,0:T(8,128)(2,1)} %copy-done), calls=%async_computation.3 | async-start | bytes 9437184 | tf_op jit(solution)/shard_map/cond/branch_1_fun/all_to_all | solution.py:423
  122.4 0.2 copy.21
  122.6 62.9 %all-to-all-done.3.in_ref = bf16[32,576,128]{2,1,0:T(8,128)(2,1)} async-done(((bf16[32,576,128]{2,1,0:T(8,128)(2,1)}), bf16[32,576,128]{2,1,0:T(8,128)(2,1)}, u32[]{:S(2)}, u32[]{:S(2)}) %all-to-all-start.3) | async-done | bytes 4718624 | tf_op jit(solution)/shard_map/cond/branch_1_fun/all_to_all | solution.py:423
  185.5 11.0 %unpack.3 = (bf16[1024,512]{1,0:T(8,128)(2,1)}, bf16[1024,512]{1,0:T(8,128)(2,1)}, bf16[1024,512]{1,0:T(8,128)(2,1)}, bf16[1024,512]{1,0:T(8,128)(2,1)}) custom-call(s32[256]{0:T(256)S(1)} %get-tuple-element.41.table_ref, s32[8,256]{1,0:T(8,128)S(1)} %get-tuple-element.39.start_ref, s32[1024,128]{1,0:T(8,128)S(1)} %pad.6.pos_ref, ...), custom_call_target="tpu_custom_call" | custom-call | tf_op jit(solution)/shard_map/cond/branch_1_fun/unpack/pallas_call | solution.py:424
  (2 shorter events, 0.0 us)
Async XLA Ops:
  0.6 0.7 copy-start.1
  3.2 19.9 %all-to-all-start.4 = ((s32[32,1,256]{2,1,0:T(1,128)}), s32[32,1,256]{2,1,0:T(1,128)S(1)}, u32[]{:S(2)}, u32[]{:S(2)}) async-start(s32[32,1,256]{2,1,0:T(1,128)} %copy.19), calls=%async_computation.4 | async-start | bytes 65536 | tf_op jit(solution)/shard_map/all_to_all | solution.py:345
  11.4 1.2 copy-start.2
  12.6 1.2 copy-start.3
  13.8 1.2 copy-start.4
  15.1 1.2 copy-start.5
  114.5 2.2 %copy-start = (bf16[32,576,128]{2,1,0:T(8,128)(2,1)}, bf16[32,576,128]{2,1,0:T(8,128)(2,1)S(1)}, u32[]{:S(2)}) copy-start(bf16[32,576,128]{2,1,0:T(8,128)(2,1)S(1)} %attend.3) | copy-start | bytes 14155780 | tf_op jit(solution)/shard_map/cond
  116.6 68.9 %all-to-all-start.3 = ((bf16[32,576,128]{2,1,0:T(8,128)(2,1)}), bf16[32,576,128]{2,1,0:T(8,128)(2,1)}, u32[]{:S(2)}, u32[]{:S(2)}) async-start(bf16[32,576,128]{2,1,0:T(8,128)(2,1)} %copy-done), calls=%async_computation.3 | async-start | bytes 9437184 | tf_op jit(solution)/shard_map/cond/branch_1_fun/all_to_all | solution.py:423

commit v3 on v2

v3 whole, which is shorter than its diff:
```python
import functools

import jax
import jax.numpy as jnp
from jax import lax
from jax.experimental import pallas as pl
from jax.experimental.pallas import tpu as pltpu
from jax.sharding import PartitionSpec as P

HEAD = 128
CLUSTERS = 64
SLOT = 24
BLOCK = 256
FIELDS = 4
TIGHT = 144
DEALS = ((0, 0, 0, 0, 0, 0), (27, 20, 16, 8, 9, 1), (2, 0, 5, 26, 20, 29), (11, 30, 23, 3, 17, 6))
CHUNKS = 4
LOG2_E = 1.4426950408889634
F32 = jnp.float32
BF16 = jnp.bfloat16
I32 = jnp.int32


def iota(shape, dim):
    return lax.broadcasted_iota(I32, shape, dim)


def against(a, b):
    return lax.dot_general(a, b, (((1,), (1,)), ((), ())), preferred_element_type=F32)


def across(a, b):
    return lax.dot_general(a, b, (((0,), (0,)), ((), ())), preferred_element_type=F32)


def limit(mib):
    return pltpu.CompilerParams(vmem_limit_bytes=mib * 1024 * 1024)


def smem():
    return pl.BlockSpec(memory_space=pltpu.SMEM)


def whole():
    return pl.BlockSpec(memory_space=pltpu.VMEM)


def outside():
    return pl.BlockSpec(memory_space=pl.ANY)


def pad_rows(capacity):
    return (capacity + SLOT + 7) // 8 * 8


def work_of(flops, moved):
    return pl.CostEstimate(flops=flops, bytes_accessed=moved, transcendentals=0)


def rank_kernel(ids_ref, pos_ref, own_ref, count_ref, start_ref):
    heads, tokens = ids_ref.shape
    pairs = heads * CLUSTERS
    marks = jnp.concatenate(
        [
            (ids_ref[h : h + 1, :] == iota((CLUSTERS, tokens), 0)).astype(BF16)
            for h in range(heads)
        ],
        axis=0,
    )
    row, col = iota((pairs, pairs), 0), iota((pairs, pairs), 1)
    earlier = ((col < row) & (col // CLUSTERS == row // CLUSTERS)).astype(BF16)
    count_wide = against(marks, jnp.ones((128, tokens), BF16))
    start_wide = jnp.dot(earlier, count_wide.astype(BF16), preferred_element_type=F32)
    count_line = against(jnp.ones((8, tokens), BF16), marks)
    own_ref[...] = count_line.astype(I32)
    for k in range(pairs // 128):
        part = count_line[None, :1, k * 128 : (k + 1) * 128].astype(I32)
        count_ref[:, k : k + 1, :] = jnp.broadcast_to(part, (count_ref.shape[0], 1, 128))
    start_ref[...] = against(count_line.astype(BF16), earlier).astype(I32)
    upper = (iota((BLOCK, BLOCK), 0) < iota((BLOCK, BLOCK), 1)).astype(BF16)
    carry = start_wide[:, :1]
    for b in range(tokens // BLOCK):
        part = marks[:, b * BLOCK : (b + 1) * BLOCK]
        before = jnp.dot(part, upper, preferred_element_type=F32) + carry
        wide = part.astype(F32)
        carry = carry + jnp.sum(wide, axis=1, keepdims=True)
        place = wide * before
        for h in range(heads):
            pos_ref[h : h + 1, b * BLOCK : (b + 1) * BLOCK] = jnp.sum(
                place[h * CLUSTERS : (h + 1) * CLUSTERS], axis=0, keepdims=True
            ).astype(I32)


def sort_kernel(pos_ref, q_ref, k_ref, v_ref, g_ref, out_ref, taken, given, in_sems, out_sems):
    heads, tokens = pos_ref.shape
    arriving = []
    for h in range(heads):
        copies = [
            pltpu.make_async_copy(
                ref.at[:, pl.ds(h * HEAD, HEAD)], taken.at[h, a], in_sems.at[h, a]
            )
            for a, ref in enumerate((q_ref, k_ref, v_ref, g_ref))
        ]
        for copy in copies:
            copy.start()
        arriving.append(copies)
    leaving = []
    for h in range(heads):
        for copy in arriving[h]:
            copy.wait()
        fields = jnp.concatenate([taken[h, a] for a in range(FIELDS)], axis=1)
        for b in range(tokens // BLOCK):
            part = slice(b * BLOCK, (b + 1) * BLOCK)
            select = (pos_ref[h : h + 1, :] == iota((BLOCK, tokens), 0) + b * BLOCK).astype(BF16)
            rows = jnp.dot(select, fields, preferred_element_type=F32).astype(BF16)
            for a in range(FIELDS):
                given[h, a, part, :] = rows[:, a * HEAD : (a + 1) * HEAD]
        copy = pltpu.make_async_copy(given.at[h], out_ref.at[h], out_sems.at[h])
        copy.start()
        leaving.append(copy)
    for copy in leaving:
        copy.wait()


def plan_kernel(padded, tokens, me_ref, from_ref, own_ref, start_ref, pack_ref, mine_ref, back_ref, most_ref):
    owners, pairs = from_ref.shape[0], own_ref.shape[1]
    rounds = pairs // owners
    deals = len(DEALS)
    counts = jnp.concatenate(
        [from_ref[:, k : k + 1, :].reshape(owners, 128) for k in range(pairs // 128)], axis=1
    )
    counts = counts.astype(F32)
    row, col = iota((pairs, pairs), 0), iota((pairs, pairs), 1)
    total_line = jnp.sum(counts, axis=0, keepdims=True)
    total_col = jnp.sum(jnp.where(row == col, total_line, 0.0), axis=1, keepdims=True)
    ahead = (total_line > total_col) | ((total_line == total_col) & (col < row))
    rank_col = jnp.sum(ahead.astype(F32), axis=1, keepdims=True)
    at_rank = rank_col == col.astype(F32)
    order_line = jnp.sum(jnp.where(at_rank, row.astype(F32), 0.0), axis=0, keepdims=True)
    size_line = jnp.sum(jnp.where(at_rank, total_col, 0.0), axis=0, keepdims=True)
    seats = deals * owners
    seat = iota((seats, 1), 0)
    device, deal = seat % owners, seat // owners
    lane = iota((seats, pairs), 1).astype(F32)
    near, far = iota((seats, seats), 0), iota((seats, seats), 1)
    together = near // owners == far // owners
    load = jnp.zeros((seats, 1), F32)
    lists = jnp.zeros((seats, 128), F32)
    owned = jnp.zeros((seats, pairs), F32)
    for r in range(rounds):
        if r >= len(DEALS[0]):
            load_line = jnp.sum(jnp.where(near == far, load, 0.0), axis=0, keepdims=True)
            lighter = (load_line < load) | ((load_line == load) & (far < near))
            turn = jnp.sum((lighter & together).astype(F32), axis=1, keepdims=True)
        else:
            shift = jnp.zeros((seats, 1), I32)
            for c in range(deals):
                shift = jnp.where(deal == c, DEALS[c][r], shift)
            turn = (device + shift) % owners
            if r % 2 == 1:
                turn = owners - 1 - turn
            turn = turn.astype(F32)
        pick = lane == turn + float(r * owners)
        item = jnp.sum(jnp.where(pick, order_line, 0.0), axis=1, keepdims=True)
        load = load + jnp.sum(jnp.where(pick, size_line, 0.0), axis=1, keepdims=True)
        lists = jnp.where(iota((seats, 128), 1) == r, item, lists)
        owned = jnp.where(lane == item, 1.0, owned)
    sent = against(counts.astype(BF16), owned.astype(BF16))
    heaviest = jnp.max(sent, axis=0, keepdims=True)
    seat_line = iota((1, seats), 1)
    least = None
    for c in range(deals):
        most = jnp.max(
            jnp.where(seat_line // owners == c, heaviest, 0.0), axis=1, keepdims=True
        )
        mine = lists[c * owners : (c + 1) * owners]
        if least is None:
            least, chosen = most, mine
        else:
            chosen = jnp.where(most < least, mine, chosen)
            least = jnp.minimum(least, most)
    most_ref[0] = jnp.max(least).astype(I32)

    lane = iota((owners, pairs), 1)
    own_line = own_ref[:1, :].astype(F32)
    begin_line = (start_ref[:1, :] + iota((1, pairs), 1) // CLUSTERS * tokens).astype(F32)
    place = jnp.zeros((owners, 1), F32)
    sources, places = jnp.zeros((owners, 128), F32), jnp.zeros((owners, 128), F32)
    back = jnp.zeros((1, pairs), F32)
    home = iota((owners, 1), 0).astype(F32) * float(padded)
    slot = iota((owners, 128), 1)
    for r in range(rounds):
        pick = lane.astype(F32) == chosen[:, r : r + 1]
        sources = jnp.where(
            slot == r, jnp.sum(jnp.where(pick, begin_line, 0.0), axis=1, keepdims=True), sources
        )
        places = jnp.where(slot == r, place, places)
        back = back + jnp.sum(jnp.where(pick, home + place, 0.0), axis=0, keepdims=True)
        place = place + jnp.sum(jnp.where(pick, own_line, 0.0), axis=1, keepdims=True)
    pack_ref[0] = sources.astype(I32)
    pack_ref[1] = places.astype(I32)
    back_ref[...] = jnp.broadcast_to(back, back_ref.shape).astype(I32)

    items = jnp.sum(jnp.where(iota((owners, 128), 0) == me_ref[0], chosen, 0.0), axis=0, keepdims=True)
    square = iota((128, 128), 0), iota((128, 128), 1)
    item_col = jnp.sum(jnp.where(square[0] == square[1], items, 0.0), axis=1, keepdims=True)
    held = (iota((128, pairs), 1).astype(F32) == item_col) & (iota((128, pairs), 0) < rounds)
    mine = against(counts.astype(BF16), held.astype(BF16)).astype(BF16)
    earlier = (square[0] < square[1]).astype(BF16)
    mine_ref[0] = jnp.dot(mine, earlier, preferred_element_type=F32).astype(I32)
    lower = (far < near)[: owners + 8, :owners].astype(BF16)
    filled = jnp.dot(lower, mine, preferred_element_type=F32).astype(I32)
    mine_ref[1] = filled[:owners]
    mine_ref[2] = jnp.broadcast_to(filled[owners : owners + 1], (owners, 128))


def pack_kernel(capacity, rounds, table_ref, sorted_ref, out_ref, taken, rows, block, given, in_sems, out_sems):
    heads, tokens = sorted_ref.shape[0], sorted_ref.shape[2]
    owners = out_ref.shape[0]
    group = owners // CHUNKS
    arriving = [
        pltpu.make_async_copy(sorted_ref.at[h], taken.at[h], in_sems.at[h]) for h in range(heads)
    ]
    for copy in arriving:
        copy.start()
    for h in range(heads):
        arriving[h].wait()
        for a in range(FIELDS):
            rows[a, h * tokens : (h + 1) * tokens, :] = taken[h, a].astype(F32)
    leaving = []
    for g in range(CHUNKS):
        part = pl.ds(g * group, group)

        def one_owner(o, _):
            d = g * group + o
            for j in range(rounds):
                source, target = table_ref[0, d, j], table_ref[1, d, j]
                for a in range(FIELDS):
                    block[a, pl.ds(target, SLOT), :] = rows[a, pl.ds(source, SLOT), :]
            for a in range(FIELDS):
                given[d, a * capacity : (a + 1) * capacity, :] = block[a, :capacity, :].astype(BF16)
            return 0

        lax.fori_loop(0, group, one_owner, 0, unroll=2)
        copy = pltpu.make_async_copy(given.at[part], out_ref.at[part], out_sems.at[g])
        copy.start()
        leaving.append(copy)
    for copy in leaving:
        copy.wait()


def attend_kernel(capacity, rounds, table_ref, in_ref, out_ref, *scratch):
    taken, given, arrived, leaving, gathered, work, done, in_sems, out_sems = scratch
    sources = in_ref.shape[0]
    group = sources // CHUNKS
    most = work.shape[1]
    factor = float(HEAD) ** -0.5
    parts = [pl.ds(g * group, group) for g in range(CHUNKS)]
    arriving = [
        pltpu.make_async_copy(in_ref.at[parts[g]], taken.at[parts[g]], in_sems.at[g])
        for g in range(CHUNKS)
    ]
    for copy in arriving:
        copy.start()

    def widen(s, _):
        for a in range(FIELDS):
            arrived[s * FIELDS + a, :capacity, :] = taken[
                s, a * capacity : (a + 1) * capacity, :
            ].astype(F32)
        return 0

    for g in range(CHUNKS):
        arriving[g].wait()
        lax.fori_loop(g * group, (g + 1) * group, widen, 0, unroll=2)

    def cluster(n):
        size = n * BLOCK
        query, keys, values, upstream = (work[a, :size, :] for a in range(FIELDS))
        scale = factor * LOG2_E
        below = iota((BLOCK, BLOCK), 0) <= iota((BLOCK, BLOCK), 1)
        keys_t = gathered[1, :size, :].T.astype(BF16)
        values_t = gathered[2, :size, :].T.astype(BF16)
        up_t = gathered[3, :size, :].T
        cols = [slice(b * BLOCK, (b + 1) * BLOCK) for b in range(n)]
        upto = [slice(0, (b + 1) * BLOCK) for b in range(n)]
        scores = [against(keys[upto[b]], query[cols[b]]) for b in range(n)]
        through = [against(values[upto[b]], upstream[cols[b]]) for b in range(n)]
        shares = []
        for b in range(n):
            s = scores[b]
            last = jnp.where(below, s[b * BLOCK :], -jnp.inf)
            s = last if b == 0 else jnp.concatenate([s[: b * BLOCK], last], axis=0)
            weights = jnp.exp2((s - jnp.max(s, axis=0, keepdims=True)) * scale)
            shares.append(weights * (1.0 / jnp.sum(weights, axis=0, keepdims=True)))
        coarse = [part.astype(BF16) for part in shares]
        attended = [
            jnp.dot(values_t[:, upto[b]], coarse[b], preferred_element_type=F32) for b in range(n)
        ]
        for b in range(n):
            done[0, cols[b], :] = attended[b].T
        for k in range(n):
            part = jnp.concatenate([coarse[b][cols[k]] for b in range(k, n)], axis=1)
            done[3, cols[k], :] = jnp.dot(part, upstream[k * BLOCK :], preferred_element_type=F32)
        slope = []
        for b in range(n):
            row_dot = jnp.sum(
                up_t[:, cols[b]] * attended[b].astype(BF16).astype(F32), axis=0, keepdims=True
            )
            slope.append((shares[b] * (through[b] - row_dot)).astype(BF16))
        for b in range(n):
            done[1, cols[b], :] = (
                factor * jnp.dot(keys_t[:, upto[b]], slope[b], preferred_element_type=F32).T
            )
        for k in range(n):
            part = jnp.concatenate([slope[b][cols[k]] for b in range(k, n)], axis=1)
            done[2, cols[k], :] = factor * jnp.dot(
                part, query[k * BLOCK :], preferred_element_type=F32
            )

    def one(j, _):
        for s in range(sources):
            place, filled = table_ref[0, s, j], table_ref[1, s, j]
            for a in range(FIELDS):
                gathered[a, pl.ds(filled, SLOT), :] = arrived[
                    s * FIELDS + a, pl.ds(place, SLOT), :
                ]
        total = table_ref[2, 0, j]
        for a in range(FIELDS):
            gathered[a, pl.ds(total, BLOCK), :] = jnp.zeros((BLOCK, HEAD), F32)
        blocks = most // BLOCK
        for n in range(1, blocks + 1):
            enough = total > (n - 1) * BLOCK
            if n < blocks:
                enough = enough & (total <= n * BLOCK)

            @pl.when(enough)
            def _():
                for a in range(FIELDS):
                    work[a, : n * BLOCK, :] = gathered[a, : n * BLOCK, :].astype(BF16)
                cluster(n)

        for s in range(sources):
            place, filled = table_ref[0, s, j], table_ref[1, s, j]
            for a in range(FIELDS):
                leaving[s * FIELDS + a, pl.ds(place, SLOT), :] = done[a, pl.ds(filled, SLOT), :]
        return 0

    lax.fori_loop(0, rounds, one, 0)

    def narrow(s, _):
        for a in range(FIELDS):
            given[s, a * capacity : (a + 1) * capacity, :] = leaving[
                s * FIELDS + a, :capacity, :
            ].astype(BF16)
        return 0

    going = []
    for g in range(CHUNKS):
        lax.fori_loop(g * group, (g + 1) * group, narrow, 0, unroll=2)
        copy = pltpu.make_async_copy(given.at[parts[g]], out_ref.at[parts[g]], out_sems.at[g])
        copy.start()
        going.append(copy)
    for copy in going:
        copy.wait()


def unpack_kernel(capacity, back_ref, start_ref, pos_ref, in_ref, *refs):
    out_refs, (taken, wide, rows, given, in_sems, out_sems) = refs[:FIELDS], refs[FIELDS:]
    owners, heads, tokens = in_ref.shape[0], given.shape[0], given.shape[2]
    padded = wide.shape[1] // owners
    group = owners // CHUNKS
    parts = [pl.ds(g * group, group) for g in range(CHUNKS)]
    arriving = [
        pltpu.make_async_copy(in_ref.at[parts[g]], taken.at[parts[g]], in_sems.at[g])
        for g in range(CHUNKS)
    ]
    for copy in arriving:
        copy.start()

    def widen(d, _):
        place = pl.multiple_of(d * padded, 8)
        for a in range(FIELDS):
            wide[a, pl.ds(place, capacity), :] = taken[
                d, a * capacity : (a + 1) * capacity, :
            ].astype(F32)
        return 0

    for g in range(CHUNKS):
        arriving[g].wait()
        lax.fori_loop(g * group, (g + 1) * group, widen, 0, unroll=2)
    leaving = []
    for h in range(heads):
        for c in range(CLUSTERS):
            target = start_ref[0, h * CLUSTERS + c]
            source = back_ref[0, h * CLUSTERS + c]
            for a in range(FIELDS):
                rows[a, pl.ds(target, SLOT), :] = wide[a, pl.ds(source, SLOT), :]
        fields = jnp.concatenate([rows[a, :tokens, :].astype(BF16) for a in range(FIELDS)], axis=1)
        for b in range(tokens // BLOCK):
            part = slice(b * BLOCK, (b + 1) * BLOCK)
            select = (pos_ref[part, h : h + 1] == iota((BLOCK, tokens), 1)).astype(BF16)
            result = jnp.dot(select, fields, preferred_element_type=F32).astype(BF16)
            for a in range(FIELDS):
                given[h, a, part, :] = result[:, a * HEAD : (a + 1) * HEAD]
        for a, ref in enumerate(out_refs):
            copy = pltpu.make_async_copy(
                given.at[h, a], ref.at[:, pl.ds(h * HEAD, HEAD)], out_sems.at[h, a]
            )
            copy.start()
            leaving.append(copy)
    for copy in leaving:
        copy.wait()


def on_device(queries, key_rows, value_rows, grad_out, cluster_ids):
    tokens, heads = cluster_ids.shape
    owners = lax.axis_size("seq")
    pairs = heads * CLUSTERS
    rounds = pairs // owners
    sorted_rows = heads * tokens + SLOT
    most = owners * SLOT
    me = lax.axis_index("seq").astype(I32).reshape(1)

    place, count, to_all, start = pl.pallas_call(
        rank_kernel,
        out_shape=(
            jax.ShapeDtypeStruct((heads, tokens), I32),
            jax.ShapeDtypeStruct((8, pairs), I32),
            jax.ShapeDtypeStruct((owners, 8, 128), I32),
            jax.ShapeDtypeStruct((8, pairs), I32),
        ),
        in_specs=[whole()],
        out_specs=(whole(),) * 4,
        compiler_params=limit(16),
        name="rank",
    )(cluster_ids.T)
    token_places = jnp.pad(place.T, ((0, 0), (0, 128 - heads)))

    from_all = lax.all_to_all(to_all, "seq", 0, 0, tiled=True)

    all_fields = pltpu.VMEM((heads, FIELDS, tokens, HEAD), BF16)
    in_order = pl.pallas_call(
        sort_kernel,
        out_shape=jax.ShapeDtypeStruct((heads, FIELDS, tokens, HEAD), BF16),
        in_specs=[whole()] + [outside()] * 4,
        out_specs=outside(),
        scratch_shapes=[
            all_fields,
            all_fields,
            pltpu.SemaphoreType.DMA((heads, FIELDS)),
            pltpu.SemaphoreType.DMA((heads,)),
        ],
        cost_estimate=work_of(
            2 * heads * tokens * tokens * FIELDS * HEAD, 4 * FIELDS * heads * tokens * HEAD
        ),
        compiler_params=limit(60),
        name="sort",
    )(place, queries, key_rows, value_rows, grad_out)

    padded = pad_rows(rounds * SLOT)
    pack_table, mine_table, back_table, heaviest = pl.pallas_call(
        functools.partial(plan_kernel, padded, tokens),
        out_shape=(
            jax.ShapeDtypeStruct((2, owners, 128), I32),
            jax.ShapeDtypeStruct((3, owners, 128), I32),
            jax.ShapeDtypeStruct((8, pairs), I32),
            jax.ShapeDtypeStruct((1,), I32),
        ),
        in_specs=[smem()] + [whole()] * 3,
        out_specs=(whole(), whole(), whole(), smem()),
        compiler_params=limit(16),
        name="plan",
    )(me, from_all, count, start)

    def exchange(capacity):
        block = (owners, FIELDS * capacity, HEAD)
        packed = jax.ShapeDtypeStruct(block, BF16)
        chunk_sems = pltpu.SemaphoreType.DMA((CHUNKS,))
        sending = pl.pallas_call(
            functools.partial(pack_kernel, capacity, rounds),
            out_shape=packed,
            in_specs=[smem(), outside()],
            out_specs=outside(),
            scratch_shapes=[
                all_fields,
                pltpu.VMEM((FIELDS, heads * tokens + SLOT, HEAD), F32),
                pltpu.VMEM((FIELDS, pad_rows(capacity), HEAD), F32),
                pltpu.VMEM(block, BF16),
                pltpu.SemaphoreType.DMA((heads,)),
                chunk_sems,
            ],
            compiler_params=limit(60),
            name="pack",
        )(pack_table, in_order)
        owned = lax.all_to_all(sending, "seq", 0, 0, tiled=True)
        results = pl.pallas_call(
            functools.partial(attend_kernel, capacity, rounds),
            out_shape=packed,
            in_specs=[smem(), outside()],
            out_specs=outside(),
            scratch_shapes=[
                pltpu.VMEM(block, BF16),
                pltpu.VMEM(block, BF16),
                pltpu.VMEM((owners * FIELDS, pad_rows(capacity), HEAD), F32),
                pltpu.VMEM((owners * FIELDS, pad_rows(capacity), HEAD), F32),
                pltpu.VMEM((FIELDS, most + BLOCK + SLOT, HEAD), F32),
                pltpu.VMEM((FIELDS, most, HEAD), BF16),
                pltpu.VMEM((FIELDS, most + SLOT, HEAD), F32),
                chunk_sems,
                chunk_sems,
            ],
            compiler_params=limit(60),
            name="attend",
        )(mine_table, owned)
        returned = lax.all_to_all(results, "seq", 0, 0, tiled=True)
        return pl.pallas_call(
            functools.partial(unpack_kernel, capacity),
            out_shape=(jax.ShapeDtypeStruct(queries.shape, BF16),) * 4,
            in_specs=[smem(), smem(), whole(), outside()],
            out_specs=(outside(),) * 4,
            scratch_shapes=[
                pltpu.VMEM(block, BF16),
                pltpu.VMEM((FIELDS, owners * padded, HEAD), F32),
                pltpu.VMEM((FIELDS, tokens + SLOT, HEAD), F32),
                all_fields,
                chunk_sems,
                pltpu.SemaphoreType.DMA((heads, FIELDS)),
            ],
            compiler_params=limit(60),
            name="unpack",
        )(back_table, start, token_places, returned)

    return lax.cond(
        heaviest[0] <= TIGHT,
        lambda: exchange(TIGHT),
        lambda: exchange(rounds * SLOT),
    )


def solution(mesh):
    spec = P("seq", "head")
    return jax.shard_map(
        on_device, mesh=mesh, in_specs=(spec,) * 5, out_specs=(spec,) * 4, check_vma=False
    )
```

time: 198 us -> 189 us (0.955)
  local copies, waits for them, and re-layouts: 9.2 us -> 1.78 us
    unnamed x11 -> x2, local copies, waits for them, and re-layouts: 5.61 us -> 0.71 us
    cond x2 -> x0, local copies, waits for them, and re-layouts: 2.16 us -> none
  transfers between devices with their start and end apart: 2 -> 2, of which waited for: 1 -> 1; matrix products, arithmetic and copies ran while one was open for 0% -> 1% of each run, Pallas kernels for 3% -> 4%
where the time goes in v3:
time: 189 us; the launch traced here: 188 us
  blocking collectives  62.5 us (33%)
  waiting for transfers between devices  62.1 us (33%)
  Pallas kernels  45.8 us (24%)
  starting transfers between devices  14 us (7%)
    all_to_all x1, blocking collectives, exchange(): owned = lax.all_to_all(sending, 'seq', 0, 0, tiled=True)  62.5 us
    all_to_all x1, waiting for transfers between devices, exchange(): returned = lax.all_to_all(results, 'seq', 0, 0, tiled=True)  62.1 us
    pallas_call x1, Pallas kernels, exchange(): pl.pallas_call(functools.partial(attend_kernel, capacity, rounds), out_sh...  19.2 us
    pallas_call x1, Pallas kernels, exchange(): pl.pallas_call(functools.partial(unpack_kernel, capacity), out_shape=(jax...  10 us
    all_to_all x1, starting transfers between devices, on_device(): from_all = lax.all_to_all(to_all, 'seq', 0, 0, tiled=True)  8.21 us
    pallas_call x1, Pallas kernels, on_device(): pl.pallas_call(sort_kernel, out_shape=jax.ShapeDtypeStruct((heads, FIELDS...  7.4 us
    pallas_call x1, Pallas kernels, exchange(): pl.pallas_call(functools.partial(pack_kernel, capacity, rounds), out_shap...  5.98 us
    all_to_all x1, starting transfers between devices, exchange(): returned = lax.all_to_all(results, 'seq', 0, 0, tiled=True)  5.75 us
  transfers between devices with their start and end apart: 2, of which 1 were waited for; matrix products, arithmetic and copies ran while one was open for 1% of the time, Pallas kernels for 4%

profile of v3, /device:TPU:34, one launch (start us, length us, event | category | flops | bytes accessed | tf_op | source)
XLA Modules:
  0.0 188.0 jit_solution(16150910783153588318)
XLA Ops:
  0.6 0.0 copy-start
  0.6 0.7 copy-done
  1.3 1.5 rank.1
  2.9 8.2 %all-to-all-start.4 = ((s32[32,8,128]{2,1,0:T(8,128)}), s32[32,8,128]{2,1,0:T(8,128)S(1)}, u32[]{:S(2)}, u32[]{:S(2)}) async-start(s32[32,8,128]{2,1,0:T(8,128)} %get-tuple-element.48), calls=%async_computation.4 | async-start | bytes 262144 | tf_op jit(solution)/shard_map/all_to_all | solution.py:440
  11.1 7.4 %sort.1 = bf16[4,4,1024,128]{3,2,1,0:T(8,128)(2,1)} custom-call(s32[4,1024]{1,0:T(4,128)S(1)} %get-tuple-element.53.pos_ref, bf16[1024,512]{1,0:T(8,128)(2,1)} %q_ref.1, bf16[1024,512]{1,0:T(8,128)(2,1)} %k_ref.1, bf16[1024,512]{1,0:T(8,128)(2,1)} %v_ref.1, bf16[1024,512]{1,0:T(8,128)(2,1)} %g_ref.1), custom_call_target="tpu_custom_call" | custom-call | flops 4294967296 | bytes 8388608 | tf_op jit(solution)/shard_map/sort/pallas_call | solution.py:443
  18.5 0.0 all-to-all-done.4.from_ref
  18.5 1.7 plan.1
  20.9 166.9 %conditional.1 = ((bf16[1024,512]{1,0:T(8,128)(2,1)}, bf16[1024,512]{1,0:T(8,128)(2,1)}, bf16[1024,512]{1,0:T(8,128)(2,1)}, bf16[1024,512]{1,0:T(8,128)(2,1)})) conditional(s32[]{:T(128)} %bitcast.2, (s32[2,32,128]{2,1,0:T(8,128)S(1)}, bf16[4,4,1024,128]{3,2,1,0:T(8,128)(2,1)}, s32[3,32,128]{2,1,0:T(8,128)S(1)}, s32[8,256]{1,0:T(8,128)S(1)}, ...), branch_computations={%region_0.1_spmd, %region_1.2_spmd} | conditional | bytes 32030764 | solution.py:534
  21.1 6.0 %pack.3 = bf16[32,576,128]{2,1,0:T(8,128)(2,1)} custom-call(s32[2,32,128]{2,1,0:T(8,128)S(1)} %get-tuple-element.34.table_ref, bf16[4,4,1024,128]{3,2,1,0:T(8,128)(2,1)} %get-tuple-element.35.sorted_ref), custom_call_target="tpu_custom_call" | custom-call | tf_op jit(solution)/shard_map/cond/branch_1_fun/pack/pallas_call | solution.py:480
  27.1 62.5 %all_to_all.22.in_ref = bf16[32,576,128]{2,1,0:T(8,128)(2,1)} all-to-all(bf16[32,576,128]{2,1,0:T(8,128)(2,1)} %pack.3), channel_id=1, replica_groups=mesh['seq'=32,'head'=4] {'seq'}, dimensions={0} | all-to-all | bytes 9437184 | tf_op jit(solution)/shard_map/cond/branch_1_fun/all_to_all | solution.py:496
  89.6 19.2 %attend.3 = bf16[32,576,128]{2,1,0:T(8,128)(2,1)} custom-call(s32[3,32,128]{2,1,0:T(8,128)S(1)} %get-tuple-element.33.table_ref, bf16[32,576,128]{2,1,0:T(8,128)(2,1)} %all_to_all.22.in_ref), custom_call_target="tpu_custom_call" | custom-call | tf_op jit(solution)/shard_map/cond/branch_1_fun/attend/pallas_call | solution.py:497
  108.8 5.8 %all-to-all-start.3 = ((bf16[32,576,128]{2,1,0:T(8,128)(2,1)}), bf16[32,576,128]{2,1,0:T(8,128)(2,1)}, u32[]{:S(2)}, u32[]{:S(2)}) async-start(bf16[32,576,128]{2,1,0:T(8,128)(2,1)} %attend.3), calls=%async_computation.3 | async-start | bytes 9437184 | tf_op jit(solution)/shard_map/cond/branch_1_fun/all_to_all | solution.py:516
  114.6 0.2 copy.18
  114.8 0.9 pad.6.pos_ref
  115.6 62.1 %all-to-all-done.3.in_ref = bf16[32,576,128]{2,1,0:T(8,128)(2,1)} async-done(((bf16[32,576,128]{2,1,0:T(8,128)(2,1)}), bf16[32,576,128]{2,1,0:T(8,128)(2,1)}, u32[]{:S(2)}, u32[]{:S(2)}) %all-to-all-start.3) | async-done | bytes 4718624 | tf_op jit(solution)/shard_map/cond/branch_1_fun/all_to_all | solution.py:516
  177.7 10.0 %unpack.3 = (bf16[1024,512]{1,0:T(8,128)(2,1)}, bf16[1024,512]{1,0:T(8,128)(2,1)}, bf16[1024,512]{1,0:T(8,128)(2,1)}, bf16[1024,512]{1,0:T(8,128)(2,1)}) custom-call(s32[8,256]{1,0:T(8,128)S(1)} %get-tuple-element.30.back_ref, s32[8,256]{1,0:T(8,128)S(1)} %get-tuple-element.31.start_ref, s32[1024,128]{1,0:T(8,128)} %pad.6.pos_ref, ...), custom_call_target="tpu_custom_call" | custom-call | tf_op jit(solution)/shard_map/cond/branch_1_fun/unpack/pallas_call | solution.py:517
Async XLA Ops:
  0.6 0.7 copy-start
  2.9 15.6 %all-to-all-start.4 = ((s32[32,8,128]{2,1,0:T(8,128)}), s32[32,8,128]{2,1,0:T(8,128)S(1)}, u32[]{:S(2)}, u32[]{:S(2)}) async-start(s32[32,8,128]{2,1,0:T(8,128)} %get-tuple-element.48), calls=%async_computation.4 | async-start | bytes 262144 | tf_op jit(solution)/shard_map/all_to_all | solution.py:440
  108.8 69.0 %all-to-all-start.3 = ((bf16[32,576,128]{2,1,0:T(8,128)(2,1)}), bf16[32,576,128]{2,1,0:T(8,128)(2,1)}, u32[]{:S(2)}, u32[]{:S(2)}) async-start(bf16[32,576,128]{2,1,0:T(8,128)(2,1)} %attend.3), calls=%async_computation.3 | async-start | bytes 9437184 | tf_op jit(solution)/shard_map/cond/branch_1_fun/all_to_all | solution.py:516

commit v4 on v3

--- a/solution.py
+++ b/solution.py
@@ -14,7 +14,6 @@
 FIELDS = 4
 TIGHT = 144
 DEALS = ((0, 0, 0, 0, 0, 0), (27, 20, 16, 8, 9, 1), (2, 0, 5, 26, 20, 29), (11, 30, 23, 3, 17, 6))
-CHUNKS = 4
 LOG2_E = 1.4426950408889634
 F32 = jnp.float32
 BF16 = jnp.bfloat16
@@ -57,7 +56,7 @@
     return pl.CostEstimate(flops=flops, bytes_accessed=moved, transcendentals=0)
 
 
-def rank_kernel(ids_ref, pos_ref, own_ref, count_ref, start_ref):
+def rank_kernel(ids_ref, pos_ref, column_ref, own_ref, count_ref, start_ref):
     heads, tokens = ids_ref.shape
     pairs = heads * CLUSTERS
     marks = jnp.concatenate(
@@ -85,10 +84,17 @@
         wide = part.astype(F32)
         carry = carry + jnp.sum(wide, axis=1, keepdims=True)
         place = wide * before
-        for h in range(heads):
-            pos_ref[h : h + 1, b * BLOCK : (b + 1) * BLOCK] = jnp.sum(
-                place[h * CLUSTERS : (h + 1) * CLUSTERS], axis=0, keepdims=True
-            ).astype(I32)
+        lines = jnp.concatenate(
+            [
+                jnp.sum(place[h * CLUSTERS : (h + 1) * CLUSTERS], axis=0, keepdims=True)
+                for h in range(heads)
+            ]
+            + [jnp.zeros((128 - heads, BLOCK), F32)],
+            axis=0,
+        )
+        part = slice(b * BLOCK, (b + 1) * BLOCK)
+        pos_ref[:, part] = lines[:heads].astype(I32)
+        column_ref[part, :] = lines.T.astype(I32)
 
 
 def sort_kernel(pos_ref, q_ref, k_ref, v_ref, g_ref, out_ref, taken, given, in_sems, out_sems):
@@ -214,10 +220,9 @@
     mine_ref[2] = jnp.broadcast_to(filled[owners : owners + 1], (owners, 128))
 
 
-def pack_kernel(capacity, rounds, table_ref, sorted_ref, out_ref, taken, rows, block, given, in_sems, out_sems):
+def pack_kernel(capacity, rounds, table_ref, sorted_ref, out_ref, taken, rows, block, in_sems):
     heads, tokens = sorted_ref.shape[0], sorted_ref.shape[2]
     owners = out_ref.shape[0]
-    group = owners // CHUNKS
     arriving = [
         pltpu.make_async_copy(sorted_ref.at[h], taken.at[h], in_sems.at[h]) for h in range(heads)
     ]
@@ -227,52 +232,33 @@
         arriving[h].wait()
         for a in range(FIELDS):
             rows[a, h * tokens : (h + 1) * tokens, :] = taken[h, a].astype(F32)
-    leaving = []
-    for g in range(CHUNKS):
-        part = pl.ds(g * group, group)
-
-        def one_owner(o, _):
-            d = g * group + o
-            for j in range(rounds):
-                source, target = table_ref[0, d, j], table_ref[1, d, j]
-                for a in range(FIELDS):
-                    block[a, pl.ds(target, SLOT), :] = rows[a, pl.ds(source, SLOT), :]
+
+    def one_owner(d, _):
+        for j in range(rounds):
+            source, target = table_ref[0, d, j], table_ref[1, d, j]
             for a in range(FIELDS):
-                given[d, a * capacity : (a + 1) * capacity, :] = block[a, :capacity, :].astype(BF16)
-            return 0
-
-        lax.fori_loop(0, group, one_owner, 0, unroll=2)
-        copy = pltpu.make_async_copy(given.at[part], out_ref.at[part], out_sems.at[g])
-        copy.start()
-        leaving.append(copy)
-    for copy in leaving:
-        copy.wait()
+                block[a, pl.ds(target, SLOT), :] = rows[a, pl.ds(source, SLOT), :]
+        for a in range(FIELDS):
+            out_ref[d, a * capacity : (a + 1) * capacity, :] = block[a, :capacity, :].astype(BF16)
+        return 0
+
+    lax.fori_loop(0, owners, one_owner, 0, unroll=2)
 
 
 def attend_kernel(capacity, rounds, table_ref, in_ref, out_ref, *scratch):
-    taken, given, arrived, leaving, gathered, work, done, in_sems, out_sems = scratch
+    arrived, leaving, gathered, work, done = scratch
     sources = in_ref.shape[0]
-    group = sources // CHUNKS
     most = work.shape[1]
     factor = float(HEAD) ** -0.5
-    parts = [pl.ds(g * group, group) for g in range(CHUNKS)]
-    arriving = [
-        pltpu.make_async_copy(in_ref.at[parts[g]], taken.at[parts[g]], in_sems.at[g])
-        for g in range(CHUNKS)
-    ]
-    for copy in arriving:
-        copy.start()
 
     def widen(s, _):
         for a in range(FIELDS):
-            arrived[s * FIELDS + a, :capacity, :] = taken[
+            arrived[s * FIELDS + a, :capacity, :] = in_ref[
                 s, a * capacity : (a + 1) * capacity, :
             ].astype(F32)
         return 0
 
-    for g in range(CHUNKS):
-        arriving[g].wait()
-        lax.fori_loop(g * group, (g + 1) * group, widen, 0, unroll=2)
+    lax.fori_loop(0, sources, widen, 0, unroll=2)
 
     def cluster(n):
         size = n * BLOCK
@@ -350,45 +336,28 @@
 
     def narrow(s, _):
         for a in range(FIELDS):
-            given[s, a * capacity : (a + 1) * capacity, :] = leaving[
+            out_ref[s, a * capacity : (a + 1) * capacity, :] = leaving[
                 s * FIELDS + a, :capacity, :
             ].astype(BF16)
         return 0
 
-    going = []
-    for g in range(CHUNKS):
-        lax.fori_loop(g * group, (g + 1) * group, narrow, 0, unroll=2)
-        copy = pltpu.make_async_copy(given.at[parts[g]], out_ref.at[parts[g]], out_sems.at[g])
-        copy.start()
-        going.append(copy)
-    for copy in going:
-        copy.wait()
+    lax.fori_loop(0, sources, narrow, 0, unroll=2)
 
 
 def unpack_kernel(capacity, back_ref, start_ref, pos_ref, in_ref, *refs):
-    out_refs, (taken, wide, rows, given, in_sems, out_sems) = refs[:FIELDS], refs[FIELDS:]
+    out_refs, (wide, rows, given, out_sems) = refs[:FIELDS], refs[FIELDS:]
     owners, heads, tokens = in_ref.shape[0], given.shape[0], given.shape[2]
     padded = wide.shape[1] // owners
-    group = owners // CHUNKS
-    parts = [pl.ds(g * group, group) for g in range(CHUNKS)]
-    arriving = [
-        pltpu.make_async_copy(in_ref.at[parts[g]], taken.at[parts[g]], in_sems.at[g])
-        for g in range(CHUNKS)
-    ]
-    for copy in arriving:
-        copy.start()
 
     def widen(d, _):
         place = pl.multiple_of(d * padded, 8)
         for a in range(FIELDS):
-            wide[a, pl.ds(place, capacity), :] = taken[
+            wide[a, pl.ds(place, capacity), :] = in_ref[
                 d, a * capacity : (a + 1) * capacity, :
             ].astype(F32)
         return 0
 
-    for g in range(CHUNKS):
-        arriving[g].wait()
-        lax.fori_loop(g * group, (g + 1) * group, widen, 0, unroll=2)
+    lax.fori_loop(0, owners, widen, 0, unroll=2)
     leaving = []
     for h in range(heads):
         for c in range(CLUSTERS):
@@ -422,20 +391,20 @@
     most = owners * SLOT
     me = lax.axis_index("seq").astype(I32).reshape(1)
 
-    place, count, to_all, start = pl.pallas_call(
+    place, token_places, count, to_all, start = pl.pallas_call(
         rank_kernel,
         out_shape=(
             jax.ShapeDtypeStruct((heads, tokens), I32),
+            jax.ShapeDtypeStruct((tokens, 128), I32),
             jax.ShapeDtypeStruct((8, pairs), I32),
             jax.ShapeDtypeStruct((owners, 8, 128), I32),
             jax.ShapeDtypeStruct((8, pairs), I32),
         ),
         in_specs=[whole()],
-        out_specs=(whole(),) * 4,
+        out_specs=(whole(),) * 5,
         compiler_params=limit(16),
         name="rank",
     )(cluster_ids.T)
-    token_places = jnp.pad(place.T, ((0, 0), (0, 128 - heads)))
 
     from_all = lax.all_to_all(to_all, "seq", 0, 0, tiled=True)
 
@@ -454,7 +423,7 @@
         cost_estimate=work_of(
             2 * heads * tokens * tokens * FIELDS * HEAD, 4 * FIELDS * heads * tokens * HEAD
         ),
-        compiler_params=limit(60),
+        compiler_params=limit(59),
         name="sort",
     )(place, queries, key_rows, value_rows, grad_out)
 
@@ -476,58 +445,49 @@
     def exchange(capacity):
         block = (owners, FIELDS * capacity, HEAD)
         packed = jax.ShapeDtypeStruct(block, BF16)
-        chunk_sems = pltpu.SemaphoreType.DMA((CHUNKS,))
         sending = pl.pallas_call(
             functools.partial(pack_kernel, capacity, rounds),
             out_shape=packed,
             in_specs=[smem(), outside()],
-            out_specs=outside(),
+            out_specs=whole(),
             scratch_shapes=[
                 all_fields,
                 pltpu.VMEM((FIELDS, heads * tokens + SLOT, HEAD), F32),
                 pltpu.VMEM((FIELDS, pad_rows(capacity), HEAD), F32),
-                pltpu.VMEM(block, BF16),
                 pltpu.SemaphoreType.DMA((heads,)),
-                chunk_sems,
             ],
-            compiler_params=limit(60),
+            compiler_params=limit(24),
             name="pack",
         )(pack_table, in_order)
         owned = lax.all_to_all(sending, "seq", 0, 0, tiled=True)
         results = pl.pallas_call(
             functools.partial(attend_kernel, capacity, rounds),
             out_shape=packed,
-            in_specs=[smem(), outside()],
-            out_specs=outside(),
+            in_specs=[smem(), whole()],
+            out_specs=whole(),
             scratch_shapes=[
-                pltpu.VMEM(block, BF16),
-                pltpu.VMEM(block, BF16),
                 pltpu.VMEM((owners * FIELDS, pad_rows(capacity), HEAD), F32),
                 pltpu.VMEM((owners * FIELDS, pad_rows(capacity), HEAD), F32),
                 pltpu.VMEM((FIELDS, most + BLOCK + SLOT, HEAD), F32),
                 pltpu.VMEM((FIELDS, most, HEAD), BF16),
                 pltpu.VMEM((FIELDS, most + SLOT, HEAD), F32),
-                chunk_sems,
-                chunk_sems,
             ],
-            compiler_params=limit(60),
+            compiler_params=limit(36 if capacity <= TIGHT else 44),
             name="attend",
         )(mine_table, owned)
         returned = lax.all_to_all(results, "seq", 0, 0, tiled=True)
         return pl.pallas_call(
             functools.partial(unpack_kernel, capacity),
             out_shape=(jax.ShapeDtypeStruct(queries.shape, BF16),) * 4,
-            in_specs=[smem(), smem(), whole(), outside()],
+            in_specs=[smem(), smem(), whole(), whole()],
             out_specs=(outside(),) * 4,
             scratch_shapes=[
-                pltpu.VMEM(block, BF16),
                 pltpu.VMEM((FIELDS, owners * padded, HEAD), F32),
                 pltpu.VMEM((FIELDS, tokens + SLOT, HEAD), F32),
                 all_fields,
-                chunk_sems,
                 pltpu.SemaphoreType.DMA((heads, FIELDS)),
             ],
-            compiler_params=limit(60),
+            compiler_params=limit(28),
             name="unpack",
         )(back_table, start, token_places, returned)
 

time: 189 us -> 176 us (0.931); the launches traced: 188 us -> 173 us
  waiting for transfers between devices: 62.1 us -> 0.01 us
  blocking collectives: 62.5 us -> 122 us
  starting transfers between devices: 14 us -> 8.21 us
  Pallas kernels: 45.8 us -> 40.1 us
    all_to_all x1 -> x0, waiting for transfers between devices: 62.1 us -> none  [exchange(): returned = lax.all_to_all(results, 'seq', 0, 0, tiled=True)]
    all_to_all x0 -> x1, blocking collectives: none -> 59.4 us  [exchange(): returned = lax.all_to_all(results, 'seq', 0, 0, tiled=True)]
    all_to_all x1 -> x0, starting transfers between devices: 5.75 us -> none  [exchange(): returned = lax.all_to_all(results, 'seq', 0, 0, tiled=True)]
    pallas_call x1, Pallas kernels: 19.2 us -> 15.9 us  [exchange(): pl.pallas_call(functools.partial(attend_kernel, capacity, rounds), out_sh...]
    pallas_call x1, Pallas kernels: 10 us -> 7.95 us  [exchange(): pl.pallas_call(functools.partial(unpack_kernel, capacity), out_shape=(jax...]
  transfers between devices with their start and end apart: 2 -> 1, of which waited for: 1 -> 0; matrix products, arithmetic and copies ran while one was open for 1% -> 0% of each run, Pallas kernels for 4% -> 5%
where the time goes in v4:
time: 176 us; the launch traced here: 173 us
  blocking collectives  122 us (69%)
  Pallas kernels  40.1 us (23%)
  starting transfers between devices  8.21 us (5%)
    all_to_all x1, blocking collectives, exchange(): owned = lax.all_to_all(sending, 'seq', 0, 0, tiled=True)  62.2 us
    all_to_all x1, blocking collectives, exchange(): returned = lax.all_to_all(results, 'seq', 0, 0, tiled=True)  59.4 us
    pallas_call x1, Pallas kernels, exchange(): pl.pallas_call(functools.partial(attend_kernel, capacity, rounds), out_sh...  15.9 us
    all_to_all x1, starting transfers between devices, on_device(): from_all = lax.all_to_all(to_all, 'seq', 0, 0, tiled=True)  8.21 us
    pallas_call x1, Pallas kernels, on_device(): pl.pallas_call(sort_kernel, out_shape=jax.ShapeDtypeStruct((heads, FIELDS...  8.1 us
    pallas_call x1, Pallas kernels, exchange(): pl.pallas_call(functools.partial(unpack_kernel, capacity), out_shape=(jax...  7.95 us
    pallas_call x1, Pallas kernels, exchange(): pl.pallas_call(functools.partial(pack_kernel, capacity, rounds), out_shap...  4.9 us
  transfers between devices with their start and end apart: 1, of which 0 were waited for; matrix products, arithmetic and copies ran while one was open for 0% of the time, Pallas kernels for 5%

profile of v4, /device:TPU:34, one launch (start us, length us, event | category | flops | bytes accessed | tf_op | source)
XLA Modules:
  0.0 173.0 jit_solution(13833342980552724832)
XLA Ops:
  0.6 0.0 copy-start
  0.6 0.7 copy-done
  1.3 1.5 rank.1
  2.9 0.0 copy-start.1
  2.9 0.6 copy-done.1
  3.5 8.2 %all-to-all-start.4 = ((s32[32,8,128]{2,1,0:T(8,128)}), s32[32,8,128]{2,1,0:T(8,128)S(1)}, u32[]{:S(2)}, u32[]{:S(2)}) async-start(s32[32,8,128]{2,1,0:T(8,128)} %get-tuple-element.49), calls=%async_computation.4 | async-start | bytes 262144 | tf_op jit(solution)/shard_map/all_to_all | solution.py:409
  11.7 8.1 %sort.1 = bf16[4,4,1024,128]{3,2,1,0:T(8,128)(2,1)} custom-call(s32[4,1024]{1,0:T(4,128)} %copy-done.1, bf16[1024,512]{1,0:T(8,128)(2,1)} %q_ref.1, bf16[1024,512]{1,0:T(8,128)(2,1)} %k_ref.1, bf16[1024,512]{1,0:T(8,128)(2,1)} %v_ref.1, bf16[1024,512]{1,0:T(8,128)(2,1)} %g_ref.1), custom_call_target="tpu_custom_call" | custom-call | flops 4294967296 | bytes 8388608 | tf_op jit(solution)/shard_map/sort/pallas_call | solution.py:412
  19.8 0.0 all-to-all-done.4.from_ref
  19.8 1.7 plan.1
  22.1 150.7 %conditional.1 = ((bf16[1024,512]{1,0:T(8,128)(2,1)}, bf16[1024,512]{1,0:T(8,128)(2,1)}, bf16[1024,512]{1,0:T(8,128)(2,1)}, bf16[1024,512]{1,0:T(8,128)(2,1)})) conditional(s32[]{:T(128)} %bitcast.2, (s32[2,32,128]{2,1,0:T(8,128)S(1)}, bf16[4,4,1024,128]{3,2,1,0:T(8,128)(2,1)}, s32[3,32,128]{2,1,0:T(8,128)S(1)}, s32[8,256]{1,0:T(8,128)S(1)}, ...), branch_computations={%region_0.0_spmd, %region_1.0_spmd} | conditional | bytes 25165832 | solution.py:494
  22.4 4.9 %pack.3 = bf16[32,576,128]{2,1,0:T(8,128)(2,1)S(1)} custom-call(s32[2,32,128]{2,1,0:T(8,128)S(1)} %get-tuple-element.34.table_ref, bf16[4,4,1024,128]{3,2,1,0:T(8,128)(2,1)} %get-tuple-element.35.sorted_ref), custom_call_target="tpu_custom_call" | custom-call | tf_op jit(solution)/shard_map/cond/branch_1_fun/pack/pallas_call | solution.py:448
  27.3 62.2 %all_to_all.23.in_ref = bf16[32,576,128]{2,1,0:T(8,128)(2,1)S(1)} all-to-all(bf16[32,576,128]{2,1,0:T(8,128)(2,1)S(1)} %pack.3), channel_id=1, replica_groups=mesh['seq'=32,'head'=4] {'seq'}, dimensions={0} | all-to-all | bytes 9437184 | tf_op jit(solution)/shard_map/cond/branch_1_fun/all_to_all | solution.py:462
  89.5 15.9 %attend.3 = bf16[32,576,128]{2,1,0:T(8,128)(2,1)S(1)} custom-call(s32[3,32,128]{2,1,0:T(8,128)S(1)} %get-tuple-element.33.table_ref, bf16[32,576,128]{2,1,0:T(8,128)(2,1)S(1)} %all_to_all.23.in_ref), custom_call_target="tpu_custom_call" | custom-call | tf_op jit(solution)/shard_map/cond/branch_1_fun/attend/pallas_call | solution.py:463
  105.4 59.4 %all_to_all.24.in_ref = bf16[32,576,128]{2,1,0:T(8,128)(2,1)S(1)} all-to-all(bf16[32,576,128]{2,1,0:T(8,128)(2,1)S(1)} %attend.3), channel_id=1, replica_groups=mesh['seq'=32,'head'=4] {'seq'}, dimensions={0} | all-to-all | bytes 9437184 | tf_op jit(solution)/shard_map/cond/branch_1_fun/all_to_all | solution.py:478
  164.8 8.0 %unpack.3 = (bf16[1024,512]{1,0:T(8,128)(2,1)}, bf16[1024,512]{1,0:T(8,128)(2,1)}, bf16[1024,512]{1,0:T(8,128)(2,1)}, bf16[1024,512]{1,0:T(8,128)(2,1)}) custom-call(s32[8,256]{1,0:T(8,128)S(1)} %get-tuple-element.30.back_ref, s32[8,256]{1,0:T(8,128)S(1)} %get-tuple-element.31.start_ref, s32[1024,128]{1,0:T(8,128)S(1)} %get-tuple-element.32.pos_ref, ...), custom_call_target="tpu_custom_call" | custom-call | tf_op jit(solution)/shard_map/cond/branch_1_fun/unpack/pallas_call | solution.py:479
Async XLA Ops:
  0.6 0.7 copy-start
  2.9 0.6 copy-start.1
  3.5 16.3 %all-to-all-start.4 = ((s32[32,8,128]{2,1,0:T(8,128)}), s32[32,8,128]{2,1,0:T(8,128)S(1)}, u32[]{:S(2)}, u32[]{:S(2)}) async-start(s32[32,8,128]{2,1,0:T(8,128)} %get-tuple-element.49), calls=%async_computation.4 | async-start | bytes 262144 | tf_op jit(solution)/shard_map/all_to_all | solution.py:409

commit v5 on v4

--- a/solution.py
+++ b/solution.py
@@ -44,8 +44,8 @@
     return pl.BlockSpec(memory_space=pltpu.VMEM)
 
 
-def outside():
-    return pl.BlockSpec(memory_space=pl.ANY)
+def in_hbm():
+    return pl.BlockSpec(memory_space=pltpu.HBM)
 
 
 def pad_rows(capacity):
@@ -56,49 +56,28 @@
     return pl.CostEstimate(flops=flops, bytes_accessed=moved, transcendentals=0)
 
 
-def rank_kernel(ids_ref, pos_ref, column_ref, own_ref, count_ref, start_ref):
+def marks_of(ids_ref):
     heads, tokens = ids_ref.shape
-    pairs = heads * CLUSTERS
-    marks = jnp.concatenate(
+    return jnp.concatenate(
         [
             (ids_ref[h : h + 1, :] == iota((CLUSTERS, tokens), 0)).astype(BF16)
             for h in range(heads)
         ],
         axis=0,
     )
-    row, col = iota((pairs, pairs), 0), iota((pairs, pairs), 1)
-    earlier = ((col < row) & (col // CLUSTERS == row // CLUSTERS)).astype(BF16)
-    count_wide = against(marks, jnp.ones((128, tokens), BF16))
-    start_wide = jnp.dot(earlier, count_wide.astype(BF16), preferred_element_type=F32)
-    count_line = against(jnp.ones((8, tokens), BF16), marks)
-    own_ref[...] = count_line.astype(I32)
-    for k in range(pairs // 128):
+
+
+def count_kernel(ids_ref, count_ref):
+    count_line = against(jnp.ones((8, ids_ref.shape[1]), BF16), marks_of(ids_ref))
+    for k in range(count_line.shape[1] // 128):
         part = count_line[None, :1, k * 128 : (k + 1) * 128].astype(I32)
         count_ref[:, k : k + 1, :] = jnp.broadcast_to(part, (count_ref.shape[0], 1, 128))
-    start_ref[...] = against(count_line.astype(BF16), earlier).astype(I32)
-    upper = (iota((BLOCK, BLOCK), 0) < iota((BLOCK, BLOCK), 1)).astype(BF16)
-    carry = start_wide[:, :1]
-    for b in range(tokens // BLOCK):
-        part = marks[:, b * BLOCK : (b + 1) * BLOCK]
-        before = jnp.dot(part, upper, preferred_element_type=F32) + carry
-        wide = part.astype(F32)
-        carry = carry + jnp.sum(wide, axis=1, keepdims=True)
-        place = wide * before
-        lines = jnp.concatenate(
-            [
-                jnp.sum(place[h * CLUSTERS : (h + 1) * CLUSTERS], axis=0, keepdims=True)
-                for h in range(heads)
-            ]
-            + [jnp.zeros((128 - heads, BLOCK), F32)],
-            axis=0,
-        )
-        part = slice(b * BLOCK, (b + 1) * BLOCK)
-        pos_ref[:, part] = lines[:heads].astype(I32)
-        column_ref[part, :] = lines.T.astype(I32)
-
-
-def sort_kernel(pos_ref, q_ref, k_ref, v_ref, g_ref, out_ref, taken, given, in_sems, out_sems):
-    heads, tokens = pos_ref.shape
+
+
+def sort_kernel(ids_ref, q_ref, k_ref, v_ref, g_ref, out_ref, place_ref, own_ref, start_ref, *scratch):
+    taken, given, in_sems, out_sems = scratch
+    heads, tokens = ids_ref.shape
+    pairs = heads * CLUSTERS
     arriving = []
     for h in range(heads):
         copies = [
@@ -110,6 +89,28 @@
         for copy in copies:
             copy.start()
         arriving.append(copies)
+
+    marks = marks_of(ids_ref)
+    row, col = iota((pairs, pairs), 0), iota((pairs, pairs), 1)
+    earlier = ((col < row) & (col // CLUSTERS == row // CLUSTERS)).astype(BF16)
+    count_wide = against(marks, jnp.ones((128, tokens), BF16))
+    start_wide = jnp.dot(earlier, count_wide.astype(BF16), preferred_element_type=F32)
+    count_line = against(jnp.ones((8, tokens), BF16), marks)
+    own_ref[...] = count_line.astype(I32)
+    start_ref[...] = against(count_line.astype(BF16), earlier).astype(I32)
+    upper = (iota((BLOCK, BLOCK), 0) < iota((BLOCK, BLOCK), 1)).astype(BF16)
+    carry = start_wide[:, :1]
+    for b in range(tokens // BLOCK):
+        part = marks[:, b * BLOCK : (b + 1) * BLOCK]
+        before = jnp.dot(part, upper, preferred_element_type=F32) + carry
+        wide = part.astype(F32)
+        carry = carry + jnp.sum(wide, axis=1, keepdims=True)
+        place = wide * before
+        for h in range(heads):
+            place_ref[h : h + 1, b * BLOCK : (b + 1) * BLOCK] = jnp.sum(
+                place[h * CLUSTERS : (h + 1) * CLUSTERS], axis=0, keepdims=True
+            ).astype(I32)
+
     leaving = []
     for h in range(heads):
         for copy in arriving[h]:
@@ -117,18 +118,21 @@
         fields = jnp.concatenate([taken[h, a] for a in range(FIELDS)], axis=1)
         for b in range(tokens // BLOCK):
             part = slice(b * BLOCK, (b + 1) * BLOCK)
-            select = (pos_ref[h : h + 1, :] == iota((BLOCK, tokens), 0) + b * BLOCK).astype(BF16)
+            select = (place_ref[h : h + 1, :] == iota((BLOCK, tokens), 0) + b * BLOCK).astype(BF16)
             rows = jnp.dot(select, fields, preferred_element_type=F32).astype(BF16)
             for a in range(FIELDS):
                 given[h, a, part, :] = rows[:, a * HEAD : (a + 1) * HEAD]
-        copy = pltpu.make_async_copy(given.at[h], out_ref.at[h], out_sems.at[h])
-        copy.start()
-        leaving.append(copy)
+            part = pl.ds(b * BLOCK, BLOCK)
+            copy = pltpu.make_async_copy(
+                given.at[h, :, part], out_ref.at[h, :, part], out_sems.at[h, b]
+            )
+            copy.start()
+            leaving.append(copy)
     for copy in leaving:
         copy.wait()
 
 
-def plan_kernel(padded, tokens, me_ref, from_ref, own_ref, start_ref, pack_ref, mine_ref, back_ref, most_ref):
+def plan(padded, tokens, me_ref, from_ref, own_ref, start_ref, pack_ref, mine_ref, back_ref, most_ref):
     owners, pairs = from_ref.shape[0], own_ref.shape[1]
     rounds = pairs // owners
     deals = len(DEALS)
@@ -220,29 +224,49 @@
     mine_ref[2] = jnp.broadcast_to(filled[owners : owners + 1], (owners, 128))
 
 
-def pack_kernel(capacity, rounds, table_ref, sorted_ref, out_ref, taken, rows, block, in_sems):
-    heads, tokens = sorted_ref.shape[0], sorted_ref.shape[2]
-    owners = out_ref.shape[0]
+def fill(capacity, rounds, table, rows, block, out_ref):
+    def one_owner(d, _):
+        for j in range(rounds):
+            source = table[0, d, j]
+            target = jnp.minimum(table[1, d, j], capacity)
+            for a in range(FIELDS):
+                block[a, pl.ds(target, SLOT), :] = rows[a, pl.ds(source, SLOT), :]
+        for a in range(FIELDS):
+            out_ref[d, a * capacity : (a + 1) * capacity, :] = block[a, :capacity, :].astype(BF16)
+        return 0
+
+    lax.fori_loop(0, out_ref.shape[0], one_owner, 0, unroll=2)
+
+
+def widen_heads(sorted_ref, rows):
+    heads, _, tokens, _ = sorted_ref.shape
+    for h in range(heads):
+        for a in range(FIELDS):
+            rows[a, h * tokens : (h + 1) * tokens, :] = sorted_ref[h, a].astype(F32)
+
+
+def pack_kernel(capacity, rounds, table_ref, sorted_ref, out_ref, rows, block):
+    widen_heads(sorted_ref, rows)
+    fill(capacity, rounds, table_ref, rows, block, out_ref)
+
+
+def plan_and_pack_kernel(capacity, rounds, padded, me_ref, from_ref, own_ref, start_ref, sorted_ref, *refs):
+    out_ref, pack_ref, mine_ref, back_ref, most_ref, taken, rows, block, table, in_sems, table_sem = refs
+    heads, _, tokens, _ = sorted_ref.shape
     arriving = [
         pltpu.make_async_copy(sorted_ref.at[h], taken.at[h], in_sems.at[h]) for h in range(heads)
     ]
     for copy in arriving:
         copy.start()
+    plan(padded, tokens, me_ref, from_ref, own_ref, start_ref, pack_ref, mine_ref, back_ref, most_ref)
+    copy = pltpu.make_async_copy(pack_ref, table, table_sem)
+    copy.start()
     for h in range(heads):
         arriving[h].wait()
         for a in range(FIELDS):
             rows[a, h * tokens : (h + 1) * tokens, :] = taken[h, a].astype(F32)
-
-    def one_owner(d, _):
-        for j in range(rounds):
-            source, target = table_ref[0, d, j], table_ref[1, d, j]
-            for a in range(FIELDS):
-                block[a, pl.ds(target, SLOT), :] = rows[a, pl.ds(source, SLOT), :]
-        for a in range(FIELDS):
-            out_ref[d, a * capacity : (a + 1) * capacity, :] = block[a, :capacity, :].astype(BF16)
-        return 0
-
-    lax.fori_loop(0, owners, one_owner, 0, unroll=2)
+    copy.wait()
+    fill(capacity, rounds, table, rows, block, out_ref)
 
 
 def attend_kernel(capacity, rounds, table_ref, in_ref, out_ref, *scratch):
@@ -262,38 +286,43 @@
 
     def cluster(n):
         size = n * BLOCK
-        query, keys, values, upstream = (work[a, :size, :] for a in range(FIELDS))
+        query, keys, values = (work[a, :size, :] for a in range(FIELDS - 1))
         scale = factor * LOG2_E
         below = iota((BLOCK, BLOCK), 0) <= iota((BLOCK, BLOCK), 1)
         keys_t = gathered[1, :size, :].T.astype(BF16)
         values_t = gathered[2, :size, :].T.astype(BF16)
         up_t = gathered[3, :size, :].T
+        upstream_t = up_t.astype(BF16)
         cols = [slice(b * BLOCK, (b + 1) * BLOCK) for b in range(n)]
         upto = [slice(0, (b + 1) * BLOCK) for b in range(n)]
         scores = [against(keys[upto[b]], query[cols[b]]) for b in range(n)]
-        through = [against(values[upto[b]], upstream[cols[b]]) for b in range(n)]
-        shares = []
+        weights, inverse = [], []
         for b in range(n):
             s = scores[b]
             last = jnp.where(below, s[b * BLOCK :], -jnp.inf)
             s = last if b == 0 else jnp.concatenate([s[: b * BLOCK], last], axis=0)
-            weights = jnp.exp2((s - jnp.max(s, axis=0, keepdims=True)) * scale)
-            shares.append(weights * (1.0 / jnp.sum(weights, axis=0, keepdims=True)))
-        coarse = [part.astype(BF16) for part in shares]
+            weights.append(jnp.exp2((s - jnp.max(s, axis=0, keepdims=True)) * scale))
+            inverse.append(1.0 / jnp.sum(weights[b], axis=0, keepdims=True))
+        coarse = [(weights[b] * inverse[b]).astype(BF16) for b in range(n)]
         attended = [
-            jnp.dot(values_t[:, upto[b]], coarse[b], preferred_element_type=F32) for b in range(n)
+            jnp.dot(values_t[:, upto[b]], coarse[b], preferred_element_type=F32)
+            for b in range(n)
         ]
         for b in range(n):
             done[0, cols[b], :] = attended[b].T
+        through = [
+            jnp.dot(values[upto[b]], upstream_t[:, cols[b]], preferred_element_type=F32)
+            for b in range(n)
+        ]
         for k in range(n):
             part = jnp.concatenate([coarse[b][cols[k]] for b in range(k, n)], axis=1)
-            done[3, cols[k], :] = jnp.dot(part, upstream[k * BLOCK :], preferred_element_type=F32)
+            done[3, cols[k], :] = against(part, upstream_t[:, k * BLOCK :])
         slope = []
         for b in range(n):
             row_dot = jnp.sum(
                 up_t[:, cols[b]] * attended[b].astype(BF16).astype(F32), axis=0, keepdims=True
             )
-            slope.append((shares[b] * (through[b] - row_dot)).astype(BF16))
+            slope.append((weights[b] * ((through[b] - row_dot) * inverse[b])).astype(BF16))
         for b in range(n):
             done[1, cols[b], :] = (
                 factor * jnp.dot(keys_t[:, upto[b]], slope[b], preferred_element_type=F32).T
@@ -306,7 +335,7 @@
 
     def one(j, _):
         for s in range(sources):
-            place, filled = table_ref[0, s, j], table_ref[1, s, j]
+            place, filled = jnp.minimum(table_ref[0, s, j], capacity), table_ref[1, s, j]
             for a in range(FIELDS):
                 gathered[a, pl.ds(filled, SLOT), :] = arrived[
                     s * FIELDS + a, pl.ds(place, SLOT), :
@@ -322,12 +351,12 @@
 
             @pl.when(enough)
             def _():
-                for a in range(FIELDS):
+                for a in range(FIELDS - 1):
                     work[a, : n * BLOCK, :] = gathered[a, : n * BLOCK, :].astype(BF16)
                 cluster(n)
 
         for s in range(sources):
-            place, filled = table_ref[0, s, j], table_ref[1, s, j]
+            place, filled = jnp.minimum(table_ref[0, s, j], capacity), table_ref[1, s, j]
             for a in range(FIELDS):
                 leaving[s * FIELDS + a, pl.ds(place, SLOT), :] = done[a, pl.ds(filled, SLOT), :]
         return 0
@@ -344,7 +373,7 @@
     lax.fori_loop(0, sources, narrow, 0, unroll=2)
 
 
-def unpack_kernel(capacity, back_ref, start_ref, pos_ref, in_ref, *refs):
+def unpack_kernel(capacity, back_ref, start_ref, place_ref, in_ref, *refs):
     out_refs, (wide, rows, given, out_sems) = refs[:FIELDS], refs[FIELDS:]
     owners, heads, tokens = in_ref.shape[0], given.shape[0], given.shape[2]
     padded = wide.shape[1] // owners
@@ -358,6 +387,10 @@
         return 0
 
     lax.fori_loop(0, owners, widen, 0, unroll=2)
+    lines = jnp.concatenate(
+        [place_ref[...].astype(F32), jnp.zeros((128 - heads, tokens), F32)], axis=0
+    )
+    columns = lines.T.astype(I32)
     leaving = []
     for h in range(heads):
         for c in range(CLUSTERS):
@@ -368,16 +401,18 @@
         fields = jnp.concatenate([rows[a, :tokens, :].astype(BF16) for a in range(FIELDS)], axis=1)
         for b in range(tokens // BLOCK):
             part = slice(b * BLOCK, (b + 1) * BLOCK)
-            select = (pos_ref[part, h : h + 1] == iota((BLOCK, tokens), 1)).astype(BF16)
+            select = (columns[part, h : h + 1] == iota((BLOCK, tokens), 1)).astype(BF16)
             result = jnp.dot(select, fields, preferred_element_type=F32).astype(BF16)
             for a in range(FIELDS):
                 given[h, a, part, :] = result[:, a * HEAD : (a + 1) * HEAD]
-        for a, ref in enumerate(out_refs):
-            copy = pltpu.make_async_copy(
-                given.at[h, a], ref.at[:, pl.ds(h * HEAD, HEAD)], out_sems.at[h, a]
-            )
-            copy.start()
-            leaving.append(copy)
+            for a, ref in enumerate(out_refs):
+                copy = pltpu.make_async_copy(
+                    given.at[h, a, pl.ds(b * BLOCK, BLOCK)],
+                    ref.at[pl.ds(b * BLOCK, BLOCK), pl.ds(h * HEAD, HEAD)],
+                    out_sems.at[h, a, b],
+                )
+                copy.start()
+                leaving.append(copy)
     for copy in leaving:
         copy.wait()
 
@@ -387,89 +422,101 @@
     owners = lax.axis_size("seq")
     pairs = heads * CLUSTERS
     rounds = pairs // owners
-    sorted_rows = heads * tokens + SLOT
     most = owners * SLOT
     me = lax.axis_index("seq").astype(I32).reshape(1)
 
-    place, token_places, count, to_all, start = pl.pallas_call(
-        rank_kernel,
+    ids = cluster_ids.T
+    padded = pad_rows(rounds * SLOT)
+    blocks = tokens // BLOCK
+    dma = pltpu.SemaphoreType.DMA
+    all_fields = pltpu.VMEM((heads, FIELDS, tokens, HEAD), BF16)
+    all_rows = pltpu.VMEM((FIELDS, heads * tokens + SLOT, HEAD), F32)
+
+    to_all = pl.pallas_call(
+        count_kernel,
+        out_shape=jax.ShapeDtypeStruct((owners, 8, 128), I32),
+        in_specs=[whole()],
+        out_specs=whole(),
+        compiler_params=limit(16),
+        name="count",
+    )(ids)
+    from_all = lax.all_to_all(to_all, "seq", 0, 0, tiled=True)
+
+    in_order, place, count, start = pl.pallas_call(
+        sort_kernel,
         out_shape=(
+            jax.ShapeDtypeStruct((heads, FIELDS, tokens, HEAD), BF16),
             jax.ShapeDtypeStruct((heads, tokens), I32),
-            jax.ShapeDtypeStruct((tokens, 128), I32),
             jax.ShapeDtypeStruct((8, pairs), I32),
-            jax.ShapeDtypeStruct((owners, 8, 128), I32),
             jax.ShapeDtypeStruct((8, pairs), I32),
         ),
-        in_specs=[whole()],
-        out_specs=(whole(),) * 5,
-        compiler_params=limit(16),
-        name="rank",
-    )(cluster_ids.T)
-
-    from_all = lax.all_to_all(to_all, "seq", 0, 0, tiled=True)
-
-    all_fields = pltpu.VMEM((heads, FIELDS, tokens, HEAD), BF16)
-    in_order = pl.pallas_call(
-        sort_kernel,
-        out_shape=jax.ShapeDtypeStruct((heads, FIELDS, tokens, HEAD), BF16),
-        in_specs=[whole()] + [outside()] * 4,
-        out_specs=outside(),
+        in_specs=[whole()] + [in_hbm()] * 4,
+        out_specs=(in_hbm(),) + (whole(),) * 3,
         scratch_shapes=[
             all_fields,
             all_fields,
-            pltpu.SemaphoreType.DMA((heads, FIELDS)),
-            pltpu.SemaphoreType.DMA((heads,)),
+            dma((heads, FIELDS)),
+            dma((heads, blocks)),
         ],
         cost_estimate=work_of(
             2 * heads * tokens * tokens * FIELDS * HEAD, 4 * FIELDS * heads * tokens * HEAD
         ),
-        compiler_params=limit(59),
+        compiler_params=limit(24),
         name="sort",
-    )(place, queries, key_rows, value_rows, grad_out)
-
-    padded = pad_rows(rounds * SLOT)
-    pack_table, mine_table, back_table, heaviest = pl.pallas_call(
-        functools.partial(plan_kernel, padded, tokens),
+    )(
+        ids,
+        *(
+            pltpu.with_memory_space_constraint(field, pltpu.HBM)
+            for field in (queries, key_rows, value_rows, grad_out)
+        ),
+    )
+
+    sending, pack_table, mine_table, back_table, heaviest = pl.pallas_call(
+        functools.partial(plan_and_pack_kernel, TIGHT, rounds, padded),
         out_shape=(
+            jax.ShapeDtypeStruct((owners, FIELDS * TIGHT, HEAD), BF16),
             jax.ShapeDtypeStruct((2, owners, 128), I32),
             jax.ShapeDtypeStruct((3, owners, 128), I32),
             jax.ShapeDtypeStruct((8, pairs), I32),
             jax.ShapeDtypeStruct((1,), I32),
         ),
-        in_specs=[smem()] + [whole()] * 3,
-        out_specs=(whole(), whole(), whole(), smem()),
-        compiler_params=limit(16),
-        name="plan",
-    )(me, from_all, count, start)
-
-    def exchange(capacity):
-        block = (owners, FIELDS * capacity, HEAD)
-        packed = jax.ShapeDtypeStruct(block, BF16)
-        sending = pl.pallas_call(
+        in_specs=[smem()] + [whole()] * 3 + [in_hbm()],
+        out_specs=(whole(),) * 4 + (smem(),),
+        scratch_shapes=[
+            all_fields,
+            all_rows,
+            pltpu.VMEM((FIELDS, pad_rows(TIGHT), HEAD), F32),
+            pltpu.SMEM((2, owners, 128), I32),
+            dma((heads,)),
+            dma(()),
+        ],
+        compiler_params=limit(24),
+        name="plan_and_pack",
+    )(me, from_all, count, start, pltpu.with_memory_space_constraint(in_order, pltpu.HBM))
+
+    def pack(capacity):
+        return pl.pallas_call(
             functools.partial(pack_kernel, capacity, rounds),
-            out_shape=packed,
-            in_specs=[smem(), outside()],
+            out_shape=jax.ShapeDtypeStruct((owners, FIELDS * capacity, HEAD), BF16),
+            in_specs=[smem(), whole()],
             out_specs=whole(),
-            scratch_shapes=[
-                all_fields,
-                pltpu.VMEM((FIELDS, heads * tokens + SLOT, HEAD), F32),
-                pltpu.VMEM((FIELDS, pad_rows(capacity), HEAD), F32),
-                pltpu.SemaphoreType.DMA((heads,)),
-            ],
+            scratch_shapes=[all_rows, pltpu.VMEM((FIELDS, pad_rows(capacity), HEAD), F32)],
             compiler_params=limit(24),
             name="pack",
         )(pack_table, in_order)
+
+    def exchange(capacity, sending):
         owned = lax.all_to_all(sending, "seq", 0, 0, tiled=True)
         results = pl.pallas_call(
             functools.partial(attend_kernel, capacity, rounds),
-            out_shape=packed,
+            out_shape=jax.ShapeDtypeStruct(owned.shape, BF16),
             in_specs=[smem(), whole()],
             out_specs=whole(),
             scratch_shapes=[
                 pltpu.VMEM((owners * FIELDS, pad_rows(capacity), HEAD), F32),
                 pltpu.VMEM((owners * FIELDS, pad_rows(capacity), HEAD), F32),
                 pltpu.VMEM((FIELDS, most + BLOCK + SLOT, HEAD), F32),
-                pltpu.VMEM((FIELDS, most, HEAD), BF16),
+                pltpu.VMEM((FIELDS - 1, most, HEAD), BF16),
                 pltpu.VMEM((FIELDS, most + SLOT, HEAD), F32),
             ],
             compiler_params=limit(36 if capacity <= TIGHT else 44),
@@ -480,22 +527,22 @@
             functools.partial(unpack_kernel, capacity),
             out_shape=(jax.ShapeDtypeStruct(queries.shape, BF16),) * 4,
             in_specs=[smem(), smem(), whole(), whole()],
-            out_specs=(outside(),) * 4,
+            out_specs=(in_hbm(),) * 4,
             scratch_shapes=[
                 pltpu.VMEM((FIELDS, owners * padded, HEAD), F32),
                 pltpu.VMEM((FIELDS, tokens + SLOT, HEAD), F32),
                 all_fields,
-                pltpu.SemaphoreType.DMA((heads, FIELDS)),
+                dma((heads, FIELDS, blocks)),
             ],
             compiler_params=limit(28),
             name="unpack",
-        )(back_table, start, token_places, returned)
-
-    return lax.cond(
-        heaviest[0] <= TIGHT,
-        lambda: exchange(TIGHT),
-        lambda: exchange(rounds * SLOT),
-    )
+        )(back_table, start, place, returned)
+
+    def again(state):
+        return (jnp.zeros((1,), I32), *exchange(rounds * SLOT, pack(rounds * SLOT)))
+
+    tight = exchange(TIGHT, sending)
+    return lax.while_loop(lambda state: state[0][0] > TIGHT, again, (heaviest, *tight))[1:]
 
 
 def solution(mesh):

time: 176 us -> 173 us (0.983)
  Pallas kernels: 40.1 us -> 37 us
    pallas_call x4 -> x3, Pallas kernels: 16.2 us -> 13.6 us  [the longest x1 7.25 us: on_device(): pl.pallas_call(sort_kernel, out_shape=(jax.ShapeDtypeStruct((heads, FIELD...]
  transfers between devices with their start and end apart: 1 -> 1, of which waited for: 0 -> 0; matrix products, arithmetic and copies ran while one was open for 0% -> 0% of each run, Pallas kernels for 5% -> 4%
where the time goes in v5:
time: 173 us; the launch traced here: 170 us
  blocking collectives  122 us (71%)
  Pallas kernels  37 us (21%)
  starting transfers between devices  8.21 us (5%)
    all_to_all x1, blocking collectives, exchange(): owned = lax.all_to_all(sending, 'seq', 0, 0, tiled=True)  62.2 us
    all_to_all x1, blocking collectives, exchange(): returned = lax.all_to_all(results, 'seq', 0, 0, tiled=True)  59.5 us
    pallas_call x1, Pallas kernels, exchange(): pl.pallas_call(functools.partial(attend_kernel, capacity, rounds), out_sh...  15.2 us
    all_to_all x1, starting transfers between devices, on_device(): from_all = lax.all_to_all(to_all, 'seq', 0, 0, tiled=True)  8.21 us
    pallas_call x1, Pallas kernels, exchange(): pl.pallas_call(functools.partial(unpack_kernel, capacity), out_shape=(jax...  8.13 us
    pallas_call x1, Pallas kernels, on_device(): pl.pallas_call(sort_kernel, out_shape=(jax.ShapeDtypeStruct((heads, FIELD...  7.25 us
    pallas_call x1, Pallas kernels, on_device(): pl.pallas_call(functools.partial(plan_and_pack_kernel, TIGHT, rounds, pad...  5.46 us
  transfers between devices with their start and end apart: 1, of which 0 were waited for; matrix products, arithmetic and copies ran while one was open for 0% of the time, Pallas kernels for 4%

profile of v5, /device:TPU:34, one launch (start us, length us, event | category | flops | bytes accessed | tf_op | source)
XLA Modules:
  0.0 169.9 jit_solution(9038624485744336329)
XLA Ops:
  0.6 0.0 copy-start.1
  0.6 0.7 copy-done.1
  1.4 0.9 count.1
  2.3 8.2 %all-to-all-start.2 = ((s32[32,8,128]{2,1,0:T(8,128)}), s32[32,8,128]{2,1,0:T(8,128)S(1)}, u32[]{:S(2)}, u32[]{:S(2)}) async-start(s32[32,8,128]{2,1,0:T(8,128)} %count.1), calls=%async_computation.2 | async-start | bytes 262144 | tf_op jit(solution)/shard_map/all_to_all | solution.py:443
  10.5 0.0 copy-start.2
  10.5 0.7 copy-done.2
  11.2 7.2 %sort.1 = (bf16[4,4,1024,128]{3,2,1,0:T(8,128)(2,1)}, s32[4,1024]{1,0:T(4,128)S(1)}, s32[8,256]{1,0:T(8,128)S(1)}, s32[8,256]{1,0:T(8,128)S(1)}) custom-call(s32[4,1024]{1,0:T(4,128)S(1)} %bitcast.4, bf16[1024,512]{1,0:T(8,128)(2,1)} %q_ref.1, bf16[1024,512]{1,0:T(8,128)(2,1)} %k_ref.1, bf16[1024,512]{1,0:T(8,128)(2,1)} %v_ref.1, bf16[1024,512]{1,0:T(8,128)(2,1)} %g_ref.1), custom_call_target="tpu_custom_call" | custom-call | flops 4294967296 | bytes 8388608 | tf_op jit(solution)/shard_map/sort/pallas_call | solution.py:445
  18.5 0.0 all-to-all-done.2.from_ref
  18.5 5.5 %plan_and_pack.1 = (bf16[32,576,128]{2,1,0:T(8,128)(2,1)S(1)}, s32[2,32,128]{2,1,0:T(8,128)S(1)}, s32[3,32,128]{2,1,0:T(8,128)S(1)}, s32[8,256]{1,0:T(8,128)S(1)}, s32[1]{0:T(128)}) custom-call(s32[1]{0:T(128)} %bitcast.1.me_ref, s32[32,8,128]{2,1,0:T(8,128)S(1)} %all-to-all-done.2.from_ref, s32[8,256]{1,0:T(8,128)S(1)} %get-tuple-element.76.own_ref, ...), custom_call_target="tpu_custom_call" | custom-call | tf_op jit(solution)/shard_map/plan_and_pack/pallas_call | solution.py:474
  24.0 62.2 %all_to_all.24.in_ref = bf16[32,576,128]{2,1,0:T(8,128)(2,1)S(1)} all-to-all(bf16[32,576,128]{2,1,0:T(8,128)(2,1)S(1)} %get-tuple-element.83), channel_id=1, replica_groups=mesh['seq'=32,'head'=4] {'seq'}, dimensions={0} | all-to-all | bytes 9437184 | tf_op jit(solution)/shard_map/all_to_all | solution.py:509
  86.2 15.2 %attend.3 = bf16[32,576,128]{2,1,0:T(8,128)(2,1)S(1)} custom-call(s32[3,32,128]{2,1,0:T(8,128)S(1)} %get-tuple-element.133.table_ref, bf16[32,576,128]{2,1,0:T(8,128)(2,1)S(1)} %all_to_all.24.in_ref), custom_call_target="tpu_custom_call" | custom-call | tf_op jit(solution)/shard_map/attend/pallas_call | solution.py:510
  101.4 59.5 %all_to_all.25.in_ref = bf16[32,576,128]{2,1,0:T(8,128)(2,1)S(1)} all-to-all(bf16[32,576,128]{2,1,0:T(8,128)(2,1)S(1)} %attend.3), channel_id=1, replica_groups=mesh['seq'=32,'head'=4] {'seq'}, dimensions={0} | all-to-all | bytes 9437184 | tf_op jit(solution)/shard_map/all_to_all | solution.py:525
  161.0 8.1 %unpack.3 = (bf16[1024,512]{1,0:T(8,128)(2,1)}, bf16[1024,512]{1,0:T(8,128)(2,1)}, bf16[1024,512]{1,0:T(8,128)(2,1)}, bf16[1024,512]{1,0:T(8,128)(2,1)}) custom-call(s32[8,256]{1,0:T(8,128)S(1)} %get-tuple-element.134.back_ref, s32[8,256]{1,0:T(8,128)S(1)} %get-tuple-element.135.start_ref, s32[4,1024]{1,0:T(4,128)S(1)} %get-tuple-element.136.place_ref, ...), custom_call_target="tpu_custom_call" | custom-call | tf_op jit(solution)/shard_map/unpack/pallas_call | solution.py:526
  169.1 0.6 while.15
Async XLA Ops:
  0.6 0.7 copy-start.1
  2.3 16.2 %all-to-all-start.2 = ((s32[32,8,128]{2,1,0:T(8,128)}), s32[32,8,128]{2,1,0:T(8,128)S(1)}, u32[]{:S(2)}, u32[]{:S(2)}) async-start(s32[32,8,128]{2,1,0:T(8,128)} %count.1), calls=%async_computation.2 | async-start | bytes 262144 | tf_op jit(solution)/shard_map/all_to_all | solution.py:443
  10.5 0.7 copy-start.2

commit v6 on v5

--- a/solution.py
+++ b/solution.py
@@ -13,7 +13,16 @@
 BLOCK = 256
 FIELDS = 4
 TIGHT = 144
-DEALS = ((0, 0, 0, 0, 0, 0), (27, 20, 16, 8, 9, 1), (2, 0, 5, 26, 20, 29), (11, 30, 23, 3, 17, 6))
+DEALS = (
+    (0, 0, 0, 0, 0, 0),
+    (27, 20, 16, 8, 9, 1),
+    (2, 0, 5, 26, 20, 29),
+    (11, 30, 23, 3, 17, 6),
+    (18, 7, 12, 31, 2, 14),
+    (5, 25, 28, 10, 19, 22),
+    (21, 13, 1, 15, 24, 4),
+    (9, 3, 30, 6, 11, 27),
+)
 LOG2_E = 1.4426950408889634
 F32 = jnp.float32
 BF16 = jnp.bfloat16
@@ -146,8 +155,8 @@
     ahead = (total_line > total_col) | ((total_line == total_col) & (col < row))
     rank_col = jnp.sum(ahead.astype(F32), axis=1, keepdims=True)
     at_rank = rank_col == col.astype(F32)
-    order_line = jnp.sum(jnp.where(at_rank, row.astype(F32), 0.0), axis=0, keepdims=True)
-    size_line = jnp.sum(jnp.where(at_rank, total_col, 0.0), axis=0, keepdims=True)
+    both_col = total_col * float(pairs) + iota((pairs, 1), 0).astype(F32)
+    both_line = jnp.sum(jnp.where(at_rank, both_col, 0.0), axis=0, keepdims=True)
     seats = deals * owners
     seat = iota((seats, 1), 0)
     device, deal = seat % owners, seat // owners
@@ -171,8 +180,10 @@
                 turn = owners - 1 - turn
             turn = turn.astype(F32)
         pick = lane == turn + float(r * owners)
-        item = jnp.sum(jnp.where(pick, order_line, 0.0), axis=1, keepdims=True)
-        load = load + jnp.sum(jnp.where(pick, size_line, 0.0), axis=1, keepdims=True)
+        both = jnp.sum(jnp.where(pick, both_line, 0.0), axis=1, keepdims=True)
+        size = jnp.floor(both * (1.0 / pairs))
+        item = both - size * float(pairs)
+        load = load + size
         lists = jnp.where(iota((seats, 128), 1) == r, item, lists)
         owned = jnp.where(lane == item, 1.0, owned)
     sent = against(counts.astype(BF16), owned.astype(BF16))
@@ -218,7 +229,7 @@
     mine = against(counts.astype(BF16), held.astype(BF16)).astype(BF16)
     earlier = (square[0] < square[1]).astype(BF16)
     mine_ref[0] = jnp.dot(mine, earlier, preferred_element_type=F32).astype(I32)
-    lower = (far < near)[: owners + 8, :owners].astype(BF16)
+    lower = (iota((owners + 8, owners), 1) < iota((owners + 8, owners), 0)).astype(BF16)
     filled = jnp.dot(lower, mine, preferred_element_type=F32).astype(I32)
     mine_ref[1] = filled[:owners]
     mine_ref[2] = jnp.broadcast_to(filled[owners : owners + 1], (owners, 128))
@@ -235,7 +246,7 @@
             out_ref[d, a * capacity : (a + 1) * capacity, :] = block[a, :capacity, :].astype(BF16)
         return 0
 
-    lax.fori_loop(0, out_ref.shape[0], one_owner, 0, unroll=2)
+    lax.fori_loop(0, out_ref.shape[0], one_owner, 0, unroll=4)
 
 
 def widen_heads(sorted_ref, rows):
@@ -282,7 +293,7 @@
             ].astype(F32)
         return 0
 
-    lax.fori_loop(0, sources, widen, 0, unroll=2)
+    lax.fori_loop(0, sources, widen, 0, unroll=8)
 
     def cluster(n):
         size = n * BLOCK
@@ -370,7 +381,7 @@
             ].astype(BF16)
         return 0
 
-    lax.fori_loop(0, sources, narrow, 0, unroll=2)
+    lax.fori_loop(0, sources, narrow, 0, unroll=8)
 
 
 def unpack_kernel(capacity, back_ref, start_ref, place_ref, in_ref, *refs):
@@ -386,7 +397,7 @@
             ].astype(F32)
         return 0
 
-    lax.fori_loop(0, owners, widen, 0, unroll=2)
+    lax.fori_loop(0, owners, widen, 0, unroll=8)
     lines = jnp.concatenate(
         [place_ref[...].astype(F32), jnp.zeros((128 - heads, tokens), F32)], axis=0
     )

time: 173 us -> 174 us (level)
  the two profiles are of different devices: /device:TPU:34 before, /device:TPU:1 now
where the time goes in v6:
time: 174 us; the launch traced here: 173 us
  blocking collectives  123 us (71%)
  Pallas kernels  36.9 us (21%)
  starting transfers between devices  9.6 us (6%)
    all_to_all x1, blocking collectives, exchange(): owned = lax.all_to_all(sending, 'seq', 0, 0, tiled=True)  63.7 us
    all_to_all x1, blocking collectives, exchange(): returned = lax.all_to_all(results, 'seq', 0, 0, tiled=True)  59.7 us
    pallas_call x1, Pallas kernels, exchange(): pl.pallas_call(functools.partial(attend_kernel, capacity, rounds), out_sh...  14.8 us
    all_to_all x1, starting transfers between devices, on_device(): from_all = lax.all_to_all(to_all, 'seq', 0, 0, tiled=True)  9.6 us
    pallas_call x1, Pallas kernels, exchange(): pl.pallas_call(functools.partial(unpack_kernel, capacity), out_shape=(jax...  8.07 us
    pallas_call x1, Pallas kernels, on_device(): pl.pallas_call(sort_kernel, out_shape=(jax.ShapeDtypeStruct((heads, FIELD...  7.24 us
    pallas_call x1, Pallas kernels, on_device(): pl.pallas_call(functools.partial(plan_and_pack_kernel, TIGHT, rounds, pad...  5.79 us
  transfers between devices with their start and end apart: 1, of which 0 were waited for; matrix products, arithmetic and copies ran while one was open for 0% of the time, Pallas kernels for 4%

profile of v6, /device:TPU:1, one launch (start us, length us, event | category | flops | bytes accessed | tf_op | source)
XLA Modules:
  0.0 173.1 jit_solution(3321816807901743397)
XLA Ops:
  0.6 0.0 copy-start.1
  0.6 0.7 copy-done.1
  1.4 0.9 count.1
  2.3 9.6 %all-to-all-start.2 = ((s32[32,8,128]{2,1,0:T(8,128)}), s32[32,8,128]{2,1,0:T(8,128)S(1)}, u32[]{:S(2)}, u32[]{:S(2)}) async-start(s32[32,8,128]{2,1,0:T(8,128)} %count.1), calls=%async_computation.2 | async-start | bytes 262144 | tf_op jit(solution)/shard_map/all_to_all | solution.py:454
  11.9 0.0 copy-start.2
  11.9 0.7 copy-done.2
  12.6 7.2 %sort.1 = (bf16[4,4,1024,128]{3,2,1,0:T(8,128)(2,1)}, s32[4,1024]{1,0:T(4,128)S(1)}, s32[8,256]{1,0:T(8,128)S(1)}, s32[8,256]{1,0:T(8,128)S(1)}) custom-call(s32[4,1024]{1,0:T(4,128)S(1)} %bitcast.4, bf16[1024,512]{1,0:T(8,128)(2,1)} %q_ref.1, bf16[1024,512]{1,0:T(8,128)(2,1)} %k_ref.1, bf16[1024,512]{1,0:T(8,128)(2,1)} %v_ref.1, bf16[1024,512]{1,0:T(8,128)(2,1)} %g_ref.1), custom_call_target="tpu_custom_call" | custom-call | flops 4294967296 | bytes 8388608 | tf_op jit(solution)/shard_map/sort/pallas_call | solution.py:456
  19.9 0.0 all-to-all-done.2.from_ref
  19.9 5.8 %plan_and_pack.1 = (bf16[32,576,128]{2,1,0:T(8,128)(2,1)S(1)}, s32[2,32,128]{2,1,0:T(8,128)S(1)}, s32[3,32,128]{2,1,0:T(8,128)S(1)}, s32[8,256]{1,0:T(8,128)S(1)}, s32[1]{0:T(128)}) custom-call(s32[1]{0:T(128)} %bitcast.1.me_ref, s32[32,8,128]{2,1,0:T(8,128)S(1)} %all-to-all-done.2.from_ref, s32[8,256]{1,0:T(8,128)S(1)} %get-tuple-element.76.own_ref, ...), custom_call_target="tpu_custom_call" | custom-call | tf_op jit(solution)/shard_map/plan_and_pack/pallas_call | solution.py:485
  25.7 63.7 %all_to_all.24.in_ref = bf16[32,576,128]{2,1,0:T(8,128)(2,1)S(1)} all-to-all(bf16[32,576,128]{2,1,0:T(8,128)(2,1)S(1)} %get-tuple-element.83), channel_id=1, replica_groups=mesh['seq'=32,'head'=4] {'seq'}, dimensions={0} | all-to-all | bytes 9437184 | tf_op jit(solution)/shard_map/all_to_all | solution.py:520
  89.4 14.8 %attend.3 = bf16[32,576,128]{2,1,0:T(8,128)(2,1)S(1)} custom-call(s32[3,32,128]{2,1,0:T(8,128)S(1)} %get-tuple-element.133.table_ref, bf16[32,576,128]{2,1,0:T(8,128)(2,1)S(1)} %all_to_all.24.in_ref), custom_call_target="tpu_custom_call" | custom-call | tf_op jit(solution)/shard_map/attend/pallas_call | solution.py:521
  104.3 59.7 %all_to_all.25.in_ref = bf16[32,576,128]{2,1,0:T(8,128)(2,1)S(1)} all-to-all(bf16[32,576,128]{2,1,0:T(8,128)(2,1)S(1)} %attend.3), channel_id=1, replica_groups=mesh['seq'=32,'head'=4] {'seq'}, dimensions={0} | all-to-all | bytes 9437184 | tf_op jit(solution)/shard_map/all_to_all | solution.py:536
  164.0 8.1 %unpack.3 = (bf16[1024,512]{1,0:T(8,128)(2,1)}, bf16[1024,512]{1,0:T(8,128)(2,1)}, bf16[1024,512]{1,0:T(8,128)(2,1)}, bf16[1024,512]{1,0:T(8,128)(2,1)}) custom-call(s32[8,256]{1,0:T(8,128)S(1)} %get-tuple-element.134.back_ref, s32[8,256]{1,0:T(8,128)S(1)} %get-tuple-element.135.start_ref, s32[4,1024]{1,0:T(4,128)S(1)} %get-tuple-element.136.place_ref, ...), custom_call_target="tpu_custom_call" | custom-call | tf_op jit(solution)/shard_map/unpack/pallas_call | solution.py:537
  172.0 0.9 while.15
Async XLA Ops:
  0.6 0.7 copy-start.1
  2.3 17.6 %all-to-all-start.2 = ((s32[32,8,128]{2,1,0:T(8,128)}), s32[32,8,128]{2,1,0:T(8,128)S(1)}, u32[]{:S(2)}, u32[]{:S(2)}) async-start(s32[32,8,128]{2,1,0:T(8,128)} %count.1), calls=%async_computation.2 | async-start | bytes 262144 | tf_op jit(solution)/shard_map/all_to_all | solution.py:454
  11.9 0.7 copy-start.2

commit v7 on v6

--- a/solution.py
+++ b/solution.py
@@ -206,40 +206,41 @@
     own_line = own_ref[:1, :].astype(F32)
     begin_line = (start_ref[:1, :] + iota((1, pairs), 1) // CLUSTERS * tokens).astype(F32)
     place = jnp.zeros((owners, 1), F32)
-    sources, places = jnp.zeros((owners, 128), F32), jnp.zeros((owners, 128), F32)
+    moves = jnp.zeros((owners, 128), F32)
     back = jnp.zeros((1, pairs), F32)
     home = iota((owners, 1), 0).astype(F32) * float(padded)
     slot = iota((owners, 128), 1)
     for r in range(rounds):
         pick = lane.astype(F32) == chosen[:, r : r + 1]
-        sources = jnp.where(
-            slot == r, jnp.sum(jnp.where(pick, begin_line, 0.0), axis=1, keepdims=True), sources
-        )
-        places = jnp.where(slot == r, place, places)
+        source = jnp.sum(jnp.where(pick, begin_line, 0.0), axis=1, keepdims=True)
+        moves = jnp.where(slot == r, source, jnp.where(slot == rounds + r, place, moves))
         back = back + jnp.sum(jnp.where(pick, home + place, 0.0), axis=0, keepdims=True)
         place = place + jnp.sum(jnp.where(pick, own_line, 0.0), axis=1, keepdims=True)
-    pack_ref[0] = sources.astype(I32)
-    pack_ref[1] = places.astype(I32)
-    back_ref[...] = jnp.broadcast_to(back, back_ref.shape).astype(I32)
+    pack_ref[...] = moves.astype(I32)
+    for k in range(pairs // 128):
+        part = slice(k * 128, (k + 1) * 128)
+        back_ref[k : k + 1, :] = back[:, part].astype(I32)
+        back_ref[pairs // 128 + k : pairs // 128 + k + 1, :] = start_ref[:1, part]
 
     items = jnp.sum(jnp.where(iota((owners, 128), 0) == me_ref[0], chosen, 0.0), axis=0, keepdims=True)
-    square = iota((128, 128), 0), iota((128, 128), 1)
-    item_col = jnp.sum(jnp.where(square[0] == square[1], items, 0.0), axis=1, keepdims=True)
-    held = (iota((128, pairs), 1).astype(F32) == item_col) & (iota((128, pairs), 0) < rounds)
+    down, right = iota((128, 128), 0), iota((128, 128), 1)
+    item_col = jnp.sum(jnp.where(right == down % rounds, items, 0.0), axis=1, keepdims=True)
+    held = (iota((128, pairs), 1).astype(F32) == item_col) & (iota((128, pairs), 0) < 3 * rounds)
     mine = against(counts.astype(BF16), held.astype(BF16)).astype(BF16)
-    earlier = (square[0] < square[1]).astype(BF16)
-    mine_ref[0] = jnp.dot(mine, earlier, preferred_element_type=F32).astype(I32)
-    lower = (iota((owners + 8, owners), 1) < iota((owners + 8, owners), 0)).astype(BF16)
-    filled = jnp.dot(lower, mine, preferred_element_type=F32).astype(I32)
-    mine_ref[1] = filled[:owners]
-    mine_ref[2] = jnp.broadcast_to(filled[owners : owners + 1], (owners, 128))
+    begin = jnp.dot(mine, (down < right).astype(BF16), preferred_element_type=F32)
+    lower = (iota((owners, owners), 1) < iota((owners, owners), 0)).astype(BF16)
+    filled = jnp.dot(lower, mine, preferred_element_type=F32)
+    total = jnp.dot(jnp.ones((owners, owners), BF16), mine, preferred_element_type=F32)
+    mine_ref[...] = jnp.where(
+        slot < rounds, begin, jnp.where(slot < 2 * rounds, filled, total)
+    ).astype(I32)
 
 
 def fill(capacity, rounds, table, rows, block, out_ref):
     def one_owner(d, _):
         for j in range(rounds):
-            source = table[0, d, j]
-            target = jnp.minimum(table[1, d, j], capacity)
+            source = table[d, j]
+            target = jnp.minimum(table[d, rounds + j], capacity)
             for a in range(FIELDS):
                 block[a, pl.ds(target, SLOT), :] = rows[a, pl.ds(source, SLOT), :]
         for a in range(FIELDS):
@@ -346,12 +347,13 @@
 
     def one(j, _):
         for s in range(sources):
-            place, filled = jnp.minimum(table_ref[0, s, j], capacity), table_ref[1, s, j]
+            place = jnp.minimum(table_ref[s, j], capacity)
+            filled = table_ref[s, rounds + j]
             for a in range(FIELDS):
                 gathered[a, pl.ds(filled, SLOT), :] = arrived[
                     s * FIELDS + a, pl.ds(place, SLOT), :
                 ]
-        total = table_ref[2, 0, j]
+        total = table_ref[0, 2 * rounds + j]
         for a in range(FIELDS):
             gathered[a, pl.ds(total, BLOCK), :] = jnp.zeros((BLOCK, HEAD), F32)
         blocks = most // BLOCK
@@ -367,7 +369,8 @@
                 cluster(n)
 
         for s in range(sources):
-            place, filled = jnp.minimum(table_ref[0, s, j], capacity), table_ref[1, s, j]
+            place = jnp.minimum(table_ref[s, j], capacity)
+            filled = table_ref[s, rounds + j]
             for a in range(FIELDS):
                 leaving[s * FIELDS + a, pl.ds(place, SLOT), :] = done[a, pl.ds(filled, SLOT), :]
         return 0
@@ -384,7 +387,7 @@
     lax.fori_loop(0, sources, narrow, 0, unroll=8)
 
 
-def unpack_kernel(capacity, back_ref, start_ref, place_ref, in_ref, *refs):
+def unpack_kernel(capacity, table_ref, place_ref, in_ref, *refs):
     out_refs, (wide, rows, given, out_sems) = refs[:FIELDS], refs[FIELDS:]
     owners, heads, tokens = in_ref.shape[0], given.shape[0], given.shape[2]
     padded = wide.shape[1] // owners
@@ -405,8 +408,9 @@
     leaving = []
     for h in range(heads):
         for c in range(CLUSTERS):
-            target = start_ref[0, h * CLUSTERS + c]
-            source = back_ref[0, h * CLUSTERS + c]
+            row, lane = divmod(h * CLUSTERS + c, 128)
+            source = table_ref[row, lane]
+            target = table_ref[heads * CLUSTERS // 128 + row, lane]
             for a in range(FIELDS):
                 rows[a, pl.ds(target, SLOT), :] = wide[a, pl.ds(source, SLOT), :]
         fields = jnp.concatenate([rows[a, :tokens, :].astype(BF16) for a in range(FIELDS)], axis=1)
@@ -486,9 +490,9 @@
         functools.partial(plan_and_pack_kernel, TIGHT, rounds, padded),
         out_shape=(
             jax.ShapeDtypeStruct((owners, FIELDS * TIGHT, HEAD), BF16),
-            jax.ShapeDtypeStruct((2, owners, 128), I32),
-            jax.ShapeDtypeStruct((3, owners, 128), I32),
-            jax.ShapeDtypeStruct((8, pairs), I32),
+            jax.ShapeDtypeStruct((owners, 128), I32),
+            jax.ShapeDtypeStruct((owners, 128), I32),
+            jax.ShapeDtypeStruct((2 * pairs // 128, 128), I32),
             jax.ShapeDtypeStruct((1,), I32),
         ),
         in_specs=[smem()] + [whole()] * 3 + [in_hbm()],
@@ -497,7 +501,7 @@
             all_fields,
             all_rows,
             pltpu.VMEM((FIELDS, pad_rows(TIGHT), HEAD), F32),
-            pltpu.SMEM((2, owners, 128), I32),
+            pltpu.SMEM((owners, 128), I32),
             dma((heads,)),
             dma(()),
         ],
@@ -537,7 +541,7 @@
         return pl.pallas_call(
             functools.partial(unpack_kernel, capacity),
             out_shape=(jax.ShapeDtypeStruct(queries.shape, BF16),) * 4,
-            in_specs=[smem(), smem(), whole(), whole()],
+            in_specs=[smem(), whole(), whole()],
             out_specs=(in_hbm(),) * 4,
             scratch_shapes=[
                 pltpu.VMEM((FIELDS, owners * padded, HEAD), F32),
@@ -547,7 +551,7 @@
             ],
             compiler_params=limit(28),
             name="unpack",
-        )(back_table, start, place, returned)
+        )(back_table, place, returned)
 
     def again(state):
         return (jnp.zeros((1,), I32), *exchange(rounds * SLOT, pack(rounds * SLOT)))

time: 174 us -> 173 us (level)
  the two profiles are of different devices: /device:TPU:1 before, /device:TPU:34 now
where the time goes in v7:
time: 173 us; the launch traced here: 170 us
  blocking collectives  122 us (71%)
  Pallas kernels  36 us (21%)
  starting transfers between devices  8.21 us (5%)
    all_to_all x1, blocking collectives, exchange(): owned = lax.all_to_all(sending, 'seq', 0, 0, tiled=True)  62.2 us
    all_to_all x1, blocking collectives, exchange(): returned = lax.all_to_all(results, 'seq', 0, 0, tiled=True)  60 us
    pallas_call x1, Pallas kernels, exchange(): pl.pallas_call(functools.partial(attend_kernel, capacity, rounds), out_sh...  14.7 us
    all_to_all x1, starting transfers between devices, on_device(): from_all = lax.all_to_all(to_all, 'seq', 0, 0, tiled=True)  8.21 us
    pallas_call x1, Pallas kernels, exchange(): pl.pallas_call(functools.partial(unpack_kernel, capacity), out_shape=(jax...  7.86 us
    pallas_call x1, Pallas kernels, on_device(): pl.pallas_call(sort_kernel, out_shape=(jax.ShapeDtypeStruct((heads, FIELD...  7.24 us
    pallas_call x1, Pallas kernels, on_device(): pl.pallas_call(functools.partial(plan_and_pack_kernel, TIGHT, rounds, pad...  5.21 us
  transfers between devices with their start and end apart: 1, of which 0 were waited for; matrix products, arithmetic and copies ran while one was open for 0% of the time, Pallas kernels for 4%

profile of v7, /device:TPU:34, one launch (start us, length us, event | category | flops | bytes accessed | tf_op | source)
XLA Modules:
  0.0 169.5 jit_solution(10950203783066915873)
XLA Ops:
  0.6 0.0 copy-start.1
  0.6 0.7 copy-done.1
  1.4 0.9 count.1
  2.3 8.2 %all-to-all-start.2 = ((s32[32,8,128]{2,1,0:T(8,128)}), s32[32,8,128]{2,1,0:T(8,128)S(1)}, u32[]{:S(2)}, u32[]{:S(2)}) async-start(s32[32,8,128]{2,1,0:T(8,128)} %count.1), calls=%async_computation.2 | async-start | bytes 262144 | tf_op jit(solution)/shard_map/all_to_all | solution.py:458
  10.5 0.0 copy-start.2
  10.5 0.7 copy-done.2
  11.2 7.2 %sort.1 = (bf16[4,4,1024,128]{3,2,1,0:T(8,128)(2,1)}, s32[4,1024]{1,0:T(4,128)S(1)}, s32[8,256]{1,0:T(8,128)S(1)}, s32[8,256]{1,0:T(8,128)S(1)}) custom-call(s32[4,1024]{1,0:T(4,128)S(1)} %bitcast.4, bf16[1024,512]{1,0:T(8,128)(2,1)} %q_ref.1, bf16[1024,512]{1,0:T(8,128)(2,1)} %k_ref.1, bf16[1024,512]{1,0:T(8,128)(2,1)} %v_ref.1, bf16[1024,512]{1,0:T(8,128)(2,1)} %g_ref.1), custom_call_target="tpu_custom_call" | custom-call | flops 4294967296 | bytes 8388608 | tf_op jit(solution)/shard_map/sort/pallas_call | solution.py:460
  18.5 0.0 all-to-all-done.2.from_ref
  18.5 5.2 %plan_and_pack.1 = (bf16[32,576,128]{2,1,0:T(8,128)(2,1)S(1)}, s32[32,128]{1,0:T(8,128)S(1)}, s32[32,128]{1,0:T(8,128)S(1)}, s32[4,128]{1,0:T(4,128)S(1)}, s32[1]{0:T(128)}) custom-call(s32[1]{0:T(128)} %bitcast.1.me_ref, s32[32,8,128]{2,1,0:T(8,128)S(1)} %all-to-all-done.2.from_ref, s32[8,256]{1,0:T(8,128)S(1)} %get-tuple-element.71.own_ref, ...), custom_call_target="tpu_custom_call" | custom-call | tf_op jit(solution)/shard_map/plan_and_pack/pallas_call | solution.py:489
  23.7 62.2 %all_to_all.24.in_ref = bf16[32,576,128]{2,1,0:T(8,128)(2,1)S(1)} all-to-all(bf16[32,576,128]{2,1,0:T(8,128)(2,1)S(1)} %get-tuple-element.78), channel_id=1, replica_groups=mesh['seq'=32,'head'=4] {'seq'}, dimensions={0} | all-to-all | bytes 9437184 | tf_op jit(solution)/shard_map/all_to_all | solution.py:524
  85.9 14.7 %attend.3 = bf16[32,576,128]{2,1,0:T(8,128)(2,1)S(1)} custom-call(s32[32,128]{1,0:T(8,128)S(1)} %get-tuple-element.125.table_ref, bf16[32,576,128]{2,1,0:T(8,128)(2,1)S(1)} %all_to_all.24.in_ref), custom_call_target="tpu_custom_call" | custom-call | tf_op jit(solution)/shard_map/attend/pallas_call | solution.py:525
  100.7 60.0 %all_to_all.25.in_ref = bf16[32,576,128]{2,1,0:T(8,128)(2,1)S(1)} all-to-all(bf16[32,576,128]{2,1,0:T(8,128)(2,1)S(1)} %attend.3), channel_id=1, replica_groups=mesh['seq'=32,'head'=4] {'seq'}, dimensions={0} | all-to-all | bytes 9437184 | tf_op jit(solution)/shard_map/all_to_all | solution.py:540
  160.6 7.9 %unpack.3 = (bf16[1024,512]{1,0:T(8,128)(2,1)}, bf16[1024,512]{1,0:T(8,128)(2,1)}, bf16[1024,512]{1,0:T(8,128)(2,1)}, bf16[1024,512]{1,0:T(8,128)(2,1)}) custom-call(s32[4,128]{1,0:T(4,128)S(1)} %get-tuple-element.126.table_ref, s32[4,1024]{1,0:T(4,128)S(1)} %get-tuple-element.127.place_ref, bf16[32,576,128]{2,1,0:T(8,128)(2,1)S(1)} %all_to_all.25.in_ref), custom_call_target="tpu_custom_call" | custom-call | tf_op jit(solution)/shard_map/unpack/pallas_call | solution.py:541
  168.5 0.9 while.15
Async XLA Ops:
  0.6 0.7 copy-start.1
  2.3 16.2 %all-to-all-start.2 = ((s32[32,8,128]{2,1,0:T(8,128)}), s32[32,8,128]{2,1,0:T(8,128)S(1)}, u32[]{:S(2)}, u32[]{:S(2)}) async-start(s32[32,8,128]{2,1,0:T(8,128)} %count.1), calls=%async_computation.2 | async-start | bytes 262144 | tf_op jit(solution)/shard_map/all_to_all | solution.py:458
  10.5 0.7 copy-start.2
